TPU v7x, 512 devices: a whole 4x8x8 slice. The times are simulated.
512 devices in a mesh: seq: 32 (over z, y_hi), fsdp: 16 (over x, y_lo, core).
Axes of the slice: x: 4, y: 8 (y_hi: 4, y_lo: 2; y = y_hi * 2 + y_lo), z: 8, core: 2. Of those that a mesh axis runs over, the one named last changes fastest.
Arguments:
- queries: bfloat16 [16, 6144, 768], P('fsdp', 'seq'), may hold values from -26 to 26
- keys: bfloat16 [16, 6144, 768], P('fsdp', 'seq'), may hold values from -26 to 26
- values: bfloat16 [16, 6144, 768], P('fsdp', 'seq'), may hold values from -6 to 6
- rec_lengths: int32 [16, 4], P('fsdp'), may hold values from 1 to 3072, 6144 in all within a row
- out_weight: bfloat16 [768, 1536], P('fsdp'), may hold values from -0.21875 to 0.21875
- cotangent: bfloat16 [16, 6144, 1536], P('fsdp', 'seq'), may hold values from -6 to 6
Outputs:
- attended: bfloat16 [16, 6144, 1536], P('fsdp', 'seq')
- grad_queries: bfloat16 [16, 6144, 768], P('fsdp', 'seq')
- grad_keys: bfloat16 [16, 6144, 768], P('fsdp', 'seq')
- grad_values: bfloat16 [16, 6144, 768], P('fsdp', 'seq')
- grad_weight: float32 [768, 1536], P('fsdp', 'seq')
Inputs may be any that keep to these rules, and one draw needn't show every extreme that they name: `rec_lengths`: each row holds 4 lengths that sum to 6144; the recordings lie end to end in frame order.
All inputs are finite; a program needn't handle non-finite values.
Results may differ from a plain program's by a relative error of at most 0.029.
Values may be sent and summed in bfloat16 or wider, within the bound.
No kernel may reach another device: no remote copies, remote signals or barrier semaphores. Data moves between devices by JAX's collectives and lax.ppermute only.
A program may use at most 128 MiB of HBM per device.

v0:
```python
import jax
import jax.numpy as jnp
from jax import lax
from jax.sharding import PartitionSpec as P

HEADS = 8
HEAD_DIM = 96
HOPS = 2


NEG_FILL = -1e30


def shifted(block, axis, distance):
    devices = range(lax.axis_size(axis))
    route = [(i - distance, i) for i in devices if i - distance in devices]
    return lax.ppermute(block, axis, route)


def allowed(query_pos, key_pos, lengths, frames, window):
    ends = jnp.cumsum(lengths)
    query_rec = jnp.sum((query_pos[:, None] >= ends[None, :-1]).astype(jnp.int32), axis=1)
    key_rec = jnp.sum((key_pos[:, None] >= ends[None, :-1]).astype(jnp.int32), axis=1)
    inside = (key_pos >= 0) & (key_pos < frames)
    near = jnp.abs(query_pos[:, None] - key_pos[None, :]) <= window
    return inside[None, :] & near & (query_rec[:, None] == key_rec[None, :])


def split_heads(matrix):
    return matrix.reshape(matrix.shape[0], HEADS, HEAD_DIM).transpose(1, 0, 2)


def merge_heads(stacked):
    return stacked.transpose(1, 0, 2).reshape(stacked.shape[1], HEADS * HEAD_DIM)


def head_forward(query_head, key_head, value_head, allowed_mask):
    scale = HEAD_DIM ** (-0.5)
    scores = jnp.dot(query_head, key_head.T, preferred_element_type=jnp.float32) * scale
    scores = jnp.where(allowed_mask, scores, NEG_FILL)
    largest = jnp.max(scores, axis=1)
    expo = jnp.where(allowed_mask, jnp.exp(scores - largest[:, None]), 0.0)
    totals = jnp.sum(expo, axis=1)
    context = (
        jnp.dot(expo.astype(jnp.bfloat16), value_head, preferred_element_type=jnp.float32)
        / totals[:, None]
    )
    return (context, largest + jnp.log(totals))


def attention_forward(query_rows, key_rows, value_rows, allowed_mask):

    def one_head(operands):
        return head_forward(operands[0], operands[1], operands[2], allowed_mask)

    context, log_total = lax.map(
        one_head, (split_heads(query_rows), split_heads(key_rows), split_heads(value_rows))
    )
    return (merge_heads(context).astype(jnp.bfloat16), log_total)


def head_grads(query_head, key_head, value_head, dcontext_head, log_total, delta, allowed_mask):
    scale = HEAD_DIM ** (-0.5)
    scores = jnp.dot(query_head, key_head.T, preferred_element_type=jnp.float32) * scale
    scores = jnp.where(allowed_mask, scores, NEG_FILL)
    probability = jnp.where(allowed_mask, jnp.exp(scores - log_total[:, None]), 0.0)
    product_grad = jnp.dot(dcontext_head, value_head.T, preferred_element_type=jnp.float32)
    score_grad = (probability * (product_grad - delta[:, None])).astype(jnp.bfloat16)
    return (probability, score_grad)


def head_backward(query_head, key_head, value_head, dcontext_head, log_total, delta, allowed_mask):
    scale = HEAD_DIM ** (-0.5)
    probability, score_grad = head_grads(
        query_head, key_head, value_head, dcontext_head, log_total, delta, allowed_mask
    )
    grad_query = jnp.dot(score_grad, key_head, preferred_element_type=jnp.float32) * scale
    grad_key = jnp.dot(score_grad.T, query_head, preferred_element_type=jnp.float32) * scale
    grad_value = jnp.dot(
        probability.astype(jnp.bfloat16).T, dcontext_head, preferred_element_type=jnp.float32
    )
    return (grad_query, grad_key, grad_value)


def attention_backward(query_rows, key_rows, value_rows, dcontext, log_total, delta, allowed_mask):

    def one_head(operands):
        return head_backward(
            operands[0],
            operands[1],
            operands[2],
            operands[3],
            operands[4],
            operands[5],
            allowed_mask,
        )

    grad_query, grad_key, grad_value = lax.map(
        one_head,
        (
            split_heads(query_rows),
            split_heads(key_rows),
            split_heads(value_rows),
            split_heads(dcontext),
            log_total,
            delta,
        ),
    )
    return (
        merge_heads(grad_query),
        jnp.concatenate([merge_heads(grad_key), merge_heads(grad_value)], axis=1),
    )


def head_delta(dcontext, context):
    product = dcontext.astype(jnp.float32) * context.astype(jnp.float32)
    return jnp.sum(product.reshape(product.shape[0], HEADS, HEAD_DIM), axis=2).T


def on_device(queries, keys, values, rec_lengths, out_weight, cotangent):
    row_count = queries.shape[1]
    inner = queries.shape[2]
    frames = row_count * lax.axis_size("seq")
    window = HOPS * row_count
    seq_index = lax.axis_index("seq")
    lengths = rec_lengths[0]
    query_rows = queries[0]
    cot_rows = cotangent[0]
    own_block = jnp.concatenate([keys[0], values[0]], axis=1)
    offsets = list(range(-HOPS, HOPS + 1))
    blocks = {0: own_block}
    lower_carry = own_block
    upper_carry = own_block
    for hop_step in range(1, HOPS + 1):
        lower_carry = shifted(lower_carry, "seq", 1)
        upper_carry = shifted(upper_carry, "seq", -1)
        blocks[-hop_step] = lower_carry
        blocks[hop_step] = upper_carry
    query_pos = seq_index * row_count + jnp.arange(row_count, dtype=jnp.int32)
    stacked = jnp.concatenate([blocks[offset] for offset in offsets], axis=0)
    stacked_pos = (seq_index - HOPS) * row_count + jnp.arange(stacked.shape[0], dtype=jnp.int32)
    stacked_mask = allowed(query_pos, stacked_pos, lengths, frames, window)
    context, log_total = attention_forward(
        query_rows, stacked[:, :inner], stacked[:, inner:], stacked_mask
    )
    attended = jnp.dot(
        context,
        lax.all_gather(out_weight, "fsdp", axis=0, tiled=True),
        preferred_element_type=jnp.float32,
    )
    dcontext = lax.dot_general(
        cot_rows,
        lax.all_gather(out_weight, "fsdp", axis=0, tiled=True),
        (((1,), (1,)), ((), ())),
        preferred_element_type=jnp.float32,
    )
    attended = attended.astype(jnp.bfloat16)
    dcontext = dcontext.astype(jnp.bfloat16)
    delta = head_delta(dcontext, context)
    grad_query = jnp.zeros((row_count, inner), jnp.float32)
    partials = {}
    for offset in offsets:
        block_rows = blocks[offset]
        block_pos = (seq_index + offset) * row_count + jnp.arange(row_count, dtype=jnp.int32)
        block_mask = allowed(query_pos, block_pos, lengths, frames, window)

        def block_terms(block_rows=block_rows, block_mask=block_mask):
            return attention_backward(
                query_rows,
                block_rows[:, :inner],
                block_rows[:, inner:],
                dcontext,
                log_total,
                delta,
                block_mask,
            )

        query_term, key_value_term = block_terms()
        grad_query = grad_query + query_term
        partials[offset] = key_value_term
    key_value_grad = partials[0]
    lower_sum = jnp.zeros((row_count, 2 * inner), jnp.float32)
    upper_sum = jnp.zeros((row_count, 2 * inner), jnp.float32)
    for hop_step in range(HOPS, 0, -1):
        lower_sum = shifted(lower_sum + partials[-hop_step], "seq", -1)
        upper_sum = shifted(upper_sum + partials[hop_step], "seq", 1)
    key_value_grad = key_value_grad + lower_sum + upper_sum
    term = lax.dot_general(
        context, cot_rows, (((0,), (0,)), ((), ())), preferred_element_type=jnp.float32
    )
    seq_total = lax.psum_scatter(
        term.astype(jnp.bfloat16), "seq", scatter_dimension=1, tiled=True
    ).astype(jnp.float32)
    grad_weight = lax.psum_scatter(seq_total, "fsdp", scatter_dimension=0, tiled=True)
    grad_keys = key_value_grad[:, :inner].astype(jnp.bfloat16)
    grad_values = key_value_grad[:, inner:].astype(jnp.bfloat16)
    return (
        attended[None],
        grad_query.astype(jnp.bfloat16)[None],
        grad_keys[None],
        grad_values[None],
        grad_weight,
    )


def solution(mesh):
    in_specs = (
        P("fsdp", "seq", None),
        P("fsdp", "seq", None),
        P("fsdp", "seq", None),
        P("fsdp", None),
        P("fsdp", None),
        P("fsdp", "seq", None),
    )
    out_specs = (
        P("fsdp", "seq", None),
        P("fsdp", "seq", None),
        P("fsdp", "seq", None),
        P("fsdp", "seq", None),
        P("fsdp", "seq"),
    )
    return jax.shard_map(
        on_device, mesh=mesh, in_specs=in_specs, out_specs=out_specs, check_vma=False
    )
```

profile of v0, /device:TPU:1, one launch (start us, length us, event | category | flops | bytes accessed | tf_op | source)
XLA Modules:
  0.0 534.5 jit_solution(10551596777544236238)
XLA Ops:
  10.8 5.9 %collective-permute-start = (bf16[192,1536]{1,0:T(8,128)(2,1)S(1)}, bf16[192,1536]{1,0:T(8,128)(2,1)}, u32[]{:S(2)}, u32[]{:S(2)}) collective-permute-start(bf16[192,1536]{1,0:T(8,128)(2,1)S(1)} %copy.114), channel_id=1, source_target_pairs={{0,16},{16,32},{32,48},{48,64},{64,80},{80,96},{96,112},{112,128},... | collective-permute-start | bytes 1769480 | tf_op jit(solution)/shard_map/ppermute | solution.py:17
  29.6 10.1 %collective-permute-start.1 = (bf16[192,1536]{1,0:T(8,128)(2,1)}, bf16[192,1536]{1,0:T(8,128)(2,1)}, u32[]{:S(2)}, u32[]{:S(2)}) collective-permute-start(bf16[192,1536]{1,0:T(8,128)(2,1)} %collective-permute-done), channel_id=1, source_target_pairs={{0,16},{16,32},{32,48},{48,64},{64,80},{80,96},{96,112},{112,128},... | collective-permute-start | bytes 1769480 | tf_op jit(solution)/shard_map/ppermute | solution.py:17
  39.7 7.4 %collective-permute-done.2 = bf16[192,1536]{1,0:T(8,128)(2,1)} collective-permute-done((bf16[192,1536]{1,0:T(8,128)(2,1)S(1)}, bf16[192,1536]{1,0:T(8,128)(2,1)}, u32[]{:S(2)}, u32[]{:S(2)}) %collective-permute-start.2) | collective-permute-done | bytes 589856 | tf_op jit(solution)/shard_map/ppermute | solution.py:17
  58.5 14.1 %collective-permute-done.1 = bf16[192,1536]{1,0:T(8,128)(2,1)} collective-permute-done((bf16[192,1536]{1,0:T(8,128)(2,1)}, bf16[192,1536]{1,0:T(8,128)(2,1)}, u32[]{:S(2)}, u32[]{:S(2)}) %collective-permute-start.1) | collective-permute-done | bytes 589856 | tf_op jit(solution)/shard_map/ppermute | solution.py:17
  72.5 2.2 copy.116
  74.8 3.9 collective-permute-done.3
  78.7 2.2 copy.119
  80.9 6.3 %concatenate.22 = bf16[960,1536]{0,1:T(8,128)(2,1)} concatenate(bf16[192,1536]{0,1:T(8,128)(2,1)} %copy.116, bf16[192,1536]{0,1:T(8,128)(2,1)S(1)} %copy.117, bf16[192,1536]{0,1:T(8,128)(2,1)S(1)} %pad_maximum_fusion.2, bf16[192,1536]{0,1:T(8,128)(2,1)S(1)} %copy.118, bf16[192,1536]{0,1:T(8,128)(2,1)} %copy.119), dimensions={0} | concatenate | bytes 5898240 | tf_op jit(solution)/shard_map/concatenate | solution.py:140
  87.2 3.9 fusion.204
  91.2 29.5 %while.88 = (s32[]{:T(128)}, bf16[8,192,96]{2,1,0:T(8,128)(2,1)S(1)}, f32[8,192]{1,0:T(8,128)S(1)}, bf16[8,192,96]{2,1,0:T(8,128)(2,1)S(1)}, bf16[8,960,96]{1,2,...) while((s32[]{:T(128)}, ...), condition=%wide.region_6.7_spmd.clone, body=%wide.region_3.6_spmd.clone.sunk | while | flops 75773760 | bytes 2844737 | solution.py:56
  128.5 2.2 convolution_convert_fusion
  131.1 2.6 convert_multiply_fusion
  136.0 32.9 %while.89 = (s32[]{:T(128)}, f32[8,192,96]{2,1,0:T(8,128)}, f32[8,192,96]{2,1,0:T(8,128)S(1)}, f32[8,192,96]{2,1,0:T(8,128)S(1)}, bf16[8,192,96]{2,1,0:T(8,128)(...) while((s32[]{:T(128)}, f32[8,192,96]{2,1,0:T(8,128)}, ...), condition=%wide.region_10.11_spmd.clone, body=%wide.region_9.10_spmd.clone.sunk | while | flops 35942400 | bytes 1440409 | solution.py:98
  170.3 2.2 reshape.289
  177.7 33.0 %while.90 = (s32[]{:T(128)}, f32[8,192,96]{2,1,0:T(8,128)}, f32[8,192,96]{2,1,0:T(8,128)S(1)}, f32[8,192,96]{2,1,0:T(8,128)S(1)}, bf16[8,192,96]{2,1,0:T(8,128)(...) while((s32[]{:T(128)}, f32[8,192,96]{2,1,0:T(8,128)}, ...), condition=%wide.region_13.14_spmd.clone, body=%wide.region_12.13_spmd.clone.sunk | while | flops 35942400 | bytes 1440409 | solution.py:98
  213.7 42.8 %while.93 = (s32[]{:T(128)}, f32[8,192,96]{2,1,0:T(8,128)}, f32[8,192,96]{2,1,0:T(8,128)}, f32[8,192,96]{2,1,0:T(8,128)}, bf16[8,192,96]{2,1,0:T(8,128)(2,1)S(1)...) while((s32[]{:T(128)}, f32[8,192,96]{2,1,0:T(8,128)}, ...), condition=%wide.region_21.22_spmd.clone, body=%wide.region_20.21_spmd.clone.sunk | while | flops 35942400 | bytes 1440409 | solution.py:98
  256.5 2.5 copy.152
  259.0 2.2 reshape.293
  261.2 2.5 copy.153
  263.7 2.2 reshape.294
  265.9 2.5 pad_maximum_fusion.1
  268.4 7.2 %collective-permute-start.6 = (f32[192,1536]{1,0:T(8,128)}, f32[192,1536]{1,0:T(8,128)}, u32[]{:S(2)}, u32[]{:S(2)}) collective-permute-start(f32[192,1536]{1,0:T(8,128)} %pad_maximum_fusion.1), channel_id=1, source_target_pairs={{0,16},{16,32},{32,48},{48,64},{64,80},{80,96},{96,112},{112,128},... | collective-permute-start | bytes 3538952 | tf_op jit(solution)/shard_map/ppermute | solution.py:17
  278.4 43.0 %while.92 = (s32[]{:T(128)}, f32[8,192,96]{2,1,0:T(8,128)}, f32[8,192,96]{2,1,0:T(8,128)}, f32[8,192,96]{2,1,0:T(8,128)}, bf16[8,192,96]{2,1,0:T(8,128)(2,1)S(1)...) while((s32[]{:T(128)}, f32[8,192,96]{2,1,0:T(8,128)}, ...), condition=%wide.region_18.19_spmd.clone, body=%wide.region_17.18_spmd.clone.sunk | while | flops 35942400 | bytes 1440409 | solution.py:98
  326.4 2.2 reshape.292
  332.0 2.8 maximum_add_fusion.1
  336.2 2.4 maximum_add_fusion.2
  338.6 6.9 %collective-permute-start.7 = (f32[192,1536]{1,0:T(8,128)}, f32[192,1536]{1,0:T(8,128)}, u32[]{:S(2)}, u32[]{:S(2)}) collective-permute-start(f32[192,1536]{1,0:T(8,128)} %maximum_add_fusion.2), channel_id=1, source_target_pairs={{0,16},{16,32},{32,48},{48,64},{64,80},{80,96},{96,112},{112,128},... | collective-permute-start | bytes 3538952 | tf_op jit(solution)/shard_map/ppermute | solution.py:17
  346.6 32.9 %while.91 = (s32[]{:T(128)}, f32[8,192,96]{2,1,0:T(8,128)}, f32[8,192,96]{2,1,0:T(8,128)S(1)}, f32[8,192,96]{2,1,0:T(8,128)S(1)}, bf16[8,192,96]{2,1,0:T(8,128)(...) while((s32[]{:T(128)}, f32[8,192,96]{2,1,0:T(8,128)}, ...), condition=%wide.region_15.16_spmd.clone, body=%wide.region_14.15_spmd.clone.sunk | while | flops 35942400 | bytes 1440393 | solution.py:98
  380.8 2.2 reshape.287
  384.6 2.4 fusion.202
  391.6 69.4 %reduce-scatter.5.cloned.1.call-done = bf16[768,48]{0,1:T(8,128)(2,1)} async-done(((bf16[768,1536]{0,1:T(8,128)(2,1)}), bf16[768,48]{0,1:T(8,128)(2,1)}) %reduce-scatter.5.cloned.1.call-update) | async-done | bytes 73744 | tf_op jit(solution)/shard_map/reduce_scatter | solution.py:191
  465.7 61.4 %reduce-scatter.7.cloned.1.call-done = f32[48,48]{1,0:T(8,128)} async-done(((f32[768,48]{1,0:T(8,128)}), f32[48,48]{1,0:T(8,128)}) %reduce-scatter.7.cloned.1.call-update) | async-done | bytes 9232
  (450 shorter events, 284.7 us)
Async XLA Ops:
  8.0 120.5 %copy-start = (bf16[1,192,1536]{2,1,0:T(8,128)(2,1)S(1)}, bf16[1,192,1536]{2,1,0:T(8,128)(2,1)}, u32[]{:S(2)}) copy-start(bf16[1,192,1536]{2,1,0:T(8,128)(2,1)} %param.23) | copy-start | bytes 1769476
  8.0 123.0 %all-gather.2.cloned.1.call-start = ((), (), s32[]{:S(2)}) async-start(), calls=%async_computation.2 | async-start | bytes 2506752 | tf_op jit(solution)/shard_map/all_gather | solution.py:148
  10.5 12.0 %copy-start.8 = (bf16[1,192,768]{2,1,0:T(8,128)(2,1)S(1)}, bf16[1,192,768]{2,1,0:T(8,128)(2,1)}, u32[]{:S(2)}) copy-start(bf16[1,192,768]{2,1,0:T(8,128)(2,1)} %param.19) | copy-start | bytes 884740
  10.5 12.4 %copy-start.9 = (bf16[1,192,768]{2,1,0:T(8,128)(2,1)S(1)}, bf16[1,192,768]{2,1,0:T(8,128)(2,1)}, u32[]{:S(2)}) copy-start(bf16[1,192,768]{2,1,0:T(8,128)(2,1)} %param.20) | copy-start | bytes 884740
  10.5 12.9 %copy-start.26 = (s32[1,4]{1,0:T(1,128)S(1)}, s32[1,4]{1,0:T(1,128)}, u32[]{:S(2)}) copy-start(s32[1,4]{1,0:T(1,128)} %param.21) | copy-start | bytes 52
  10.8 18.8 %collective-permute-start = (bf16[192,1536]{1,0:T(8,128)(2,1)S(1)}, bf16[192,1536]{1,0:T(8,128)(2,1)}, u32[]{:S(2)}, u32[]{:S(2)}) collective-permute-start(bf16[192,1536]{1,0:T(8,128)(2,1)S(1)} %copy.114), channel_id=1, source_target_pairs={{0,16},{16,32},{32,48},{48,64},{64,80},{80,96},{96,112},{112,128},... | collective-permute-start | bytes 1769480 | tf_op jit(solution)/shard_map/ppermute | solution.py:17
  16.7 30.5 %collective-permute-start.2 = (bf16[192,1536]{1,0:T(8,128)(2,1)S(1)}, bf16[192,1536]{1,0:T(8,128)(2,1)}, u32[]{:S(2)}, u32[]{:S(2)}) collective-permute-start(bf16[192,1536]{1,0:T(8,128)(2,1)S(1)} %copy.114), channel_id=1, source_target_pairs={{16,0},{32,16},{48,32},{64,48},{80,64},{96,80},{112,96},{128,112},... | collective-permute-start | bytes 1769480 | tf_op jit(solution)/shard_map/ppermute | solution.py:17
  18.0 443.0 %reduce-scatter.5.cloned.1.call-start = ((), (), s32[]{:S(2)}) async-start(), calls=%async_computation.3 | async-start | bytes 2433024 | tf_op jit(solution)/shard_map/reduce_scatter | solution.py:191
  25.6 1.9 copy-start.10
  25.6 1.9 copy-start.14
  29.6 42.9 %collective-permute-start.1 = (bf16[192,1536]{1,0:T(8,128)(2,1)}, bf16[192,1536]{1,0:T(8,128)(2,1)}, u32[]{:S(2)}, u32[]{:S(2)}) collective-permute-start(bf16[192,1536]{1,0:T(8,128)(2,1)} %collective-permute-done), channel_id=1, source_target_pairs={{0,16},{16,32},{32,48},{48,64},{64,80},{80,96},{96,112},{112,128},... | collective-permute-start | bytes 1769480 | tf_op jit(solution)/shard_map/ppermute | solution.py:17
  47.2 31.5 %collective-permute-start.3 = (bf16[192,1536]{1,0:T(8,128)(2,1)}, bf16[192,1536]{1,0:T(8,128)(2,1)}, u32[]{:S(2)}, u32[]{:S(2)}) collective-permute-start(bf16[192,1536]{1,0:T(8,128)(2,1)} %collective-permute-done.2), channel_id=1, source_target_pairs={{16,0},{32,16},{48,32},{64,48},{80,64},{96,80},{112,96},{128,112},... | collective-permute-start | bytes 1769480 | tf_op jit(solution)/shard_map/ppermute | solution.py:17
  87.2 4.0 copy-start.7
  87.2 4.0 copy-start.11
  87.2 4.0 copy-start.12
  87.2 4.0 copy-start.13
  130.8 396.3 %reduce-scatter.7.cloned.1.call-start = ((), (), s32[]{:S(2)}) async-start(), calls=%async_computation.4 | async-start | bytes 417792
  175.2 156.8 %collective-permute-start.4 = (f32[192,1536]{1,0:T(8,128)}, f32[192,1536]{1,0:T(8,128)}, u32[]{:S(2)}, u32[]{:S(2)}) collective-permute-start(f32[192,1536]{1,0:T(8,128)} %pad_maximum_fusion), channel_id=1, source_target_pairs={{16,0},{32,16},{48,32},{64,48},{80,64},{96,80},{112,96},{128,112},... | collective-permute-start | bytes 3538952 | tf_op jit(solution)/shard_map/ppermute | solution.py:17
  210.7 3.0 copy-start.17
  210.7 3.0 copy-start.23
  210.7 3.0 copy-start.29
  268.4 67.8 %collective-permute-start.6 = (f32[192,1536]{1,0:T(8,128)}, f32[192,1536]{1,0:T(8,128)}, u32[]{:S(2)}, u32[]{:S(2)}) collective-permute-start(f32[192,1536]{1,0:T(8,128)} %pad_maximum_fusion.1), channel_id=1, source_target_pairs={{0,16},{16,32},{32,48},{48,64},{64,80},{80,96},{96,112},{112,128},... | collective-permute-start | bytes 3538952 | tf_op jit(solution)/shard_map/ppermute | solution.py:17
  275.5 2.9 copy-start.15
  275.5 2.9 copy-start.22
  275.5 2.9 copy-start.28
  325.0 3.6 copy-start.3
  332.0 4.1 copy-start.4
  334.9 127.9 %collective-permute-start.5 = (f32[192,1536]{1,0:T(8,128)}, f32[192,1536]{1,0:T(8,128)}, u32[]{:S(2)}, u32[]{:S(2)}) collective-permute-start(f32[192,1536]{1,0:T(8,128)} %maximum_add_fusion.1), channel_id=1, source_target_pairs={{16,0},{32,16},{48,32},{64,48},{80,64},{96,80},{112,96},{128,112},... | collective-permute-start | bytes 3538952 | tf_op jit(solution)/shard_map/ppermute | solution.py:17
  338.6 124.2 %collective-permute-start.7 = (f32[192,1536]{1,0:T(8,128)}, f32[192,1536]{1,0:T(8,128)}, u32[]{:S(2)}, u32[]{:S(2)}) collective-permute-start(f32[192,1536]{1,0:T(8,128)} %maximum_add_fusion.2), channel_id=1, source_target_pairs={{0,16},{16,32},{32,48},{48,64},{64,80},{80,96},{96,112},{112,128},... | collective-permute-start | bytes 3538952 | tf_op jit(solution)/shard_map/ppermute | solution.py:17
  384.6 5.5 %copy-start.2 = (bf16[768,1536]{1,0:T(8,128)(2,1)S(1)}, bf16[768,1536]{1,0:T(8,128)(2,1)}, u32[]{:S(2)}) copy-start(bf16[768,1536]{1,0:T(8,128)(2,1)} %all-gather.2.cloned.1.call-done) | copy-start | bytes 7077892
  391.6 71.2 %copy-start.5 = (f32[192,768]{1,0:T(8,128)S(1)}, f32[192,768]{1,0:T(8,128)}, u32[]{:S(2)}) copy-start(f32[192,768]{1,0:T(8,128)} %reshape.287) | copy-start | bytes 1769476
  462.8 64.3 %copy-start.1 = (bf16[1,192,1536]{2,1,0:T(8,128)(2,1)S(1)}, bf16[1,192,1536]{2,1,0:T(8,128)(2,1)}, u32[]{:S(2)}) copy-start(bf16[1,192,1536]{2,1,0:T(8,128)(2,1)} %param.23) | copy-start | bytes 1769476
  (11 other events, 15.2 us)
Sparse Core Ops, SparseCore 0:
  18.1 74.3 all-gather.1
  462.9 64.1 reduce-scatter.6
Sparse Core Ops, SparseCore 1:
  130.9 330.0 reduce-scatter.4
where the time goes:
time: 544 us; the launch traced here: 535 us
  matrix products  213 us (39%)
  waiting for transfers between devices  157 us (29%)
  local copies, waits for them, and re-layouts  85.7 us (16%)
  starting transfers between devices  35.5 us (7%)
  other arithmetic  25.4 us (5%)
  between operations  16.2 us (3%)
    reduce_scatter x1, waiting for transfers between devices, on_device(): lax.psum_scatter(term.astype(jnp.bfloat16), 'seq', scatter_dimension=1, t...  69.4 us
    dot_general x40, matrix products, head_backward(): jnp.dot(score_grad, key_head, preferred_element_type=jnp.float32) * scale  64.6 us
    unnamed x4, waiting for transfers between devices  61.4 us
    dot_general x40, matrix products, head_grads(): jnp.dot(query_head, key_head.T, preferred_element_type=jnp.float32) * scale  41.1 us
    dot_general x40, matrix products, head_grads(): jnp.dot(dcontext_head, value_head.T, preferred_element_type=jnp.float32)  40.2 us
    ppermute x8, starting transfers between devices, shifted(): return lax.ppermute(block, axis, route)  35.2 us
    ppermute x8, waiting for transfers between devices, shifted(): return lax.ppermute(block, axis, route)  26.1 us
    dot_general x40, matrix products, head_backward(): jnp.dot(score_grad.T, query_head, preferred_element_type=jnp.float32)  18.7 us
  transfers between devices with their start and end apart: 11, of which 6 were waited for; matrix products, arithmetic and copies ran while one was open for 60% of the time, Pallas kernels for 0%

commit v1 on v0

v1 whole, which is shorter than its diff:
```python
import jax
import jax.numpy as jnp
from jax import lax
from jax.experimental import pallas as pl
from jax.experimental.pallas import tpu as pltpu
from jax.sharding import PartitionSpec as P

HEAD_DIM = 96
ROWS = 192
GROUP = 4
PAIR = 2 * HEAD_DIM
INNER = GROUP * PAIR
OWN = GROUP * ROWS
REACH = 2 * ROWS
SPAN = OWN + 2 * REACH
TILE = 256
WINDOW = TILE + 2 * REACH
STRIP = 48
WIDTH = 1536
SCALE = HEAD_DIM ** (-0.5)
LOG2E = 1.4426950408889634
NEG_FILL = -1e30
BF16 = jnp.bfloat16
F32 = jnp.float32


def struct(shape, dtype=BF16):
    return jax.ShapeDtypeStruct(shape, dtype)


def call(body, out_shape, args, flops=0, scratch=(), smem=1):
    vmem = pl.BlockSpec(memory_space=pltpu.VMEM)
    scalars = pl.BlockSpec(memory_space=pltpu.SMEM)
    moved = sum(a.size * a.dtype.itemsize for a in args)
    moved += sum(o.size * o.dtype.itemsize for o in jax.tree.leaves(out_shape))
    return pl.pallas_call(
        body,
        out_shape=out_shape,
        in_specs=[scalars] * smem + [vmem] * (len(args) - smem),
        out_specs=jax.tree.map(lambda _: vmem, out_shape),
        scratch_shapes=list(scratch),
        cost_estimate=pl.CostEstimate(flops=flops, bytes_accessed=moved, transcendentals=0),
        compiler_params=pltpu.CompilerParams(vmem_limit_bytes=40 * 1024 * 1024),
    )(*args)


def wrap(index):
    return lax.rem(index + 2 * GROUP, GROUP)


def rows_at(start, size):
    return pl.ds(pl.multiple_of(start, 16), size)


def dot(a, b):
    return jnp.dot(a, b, preferred_element_type=F32)


def dot_nt(a, b):
    return lax.dot_general(a, b, (((1,), (1,)), ((), ())), preferred_element_type=F32)


def pack_heads(pos, q, k, v, *outs):
    y = pos[0]
    for head_pair in range(GROUP):
        columns = slice(head_pair * PAIR, (head_pair + 1) * PAIR)
        hop = wrap(head_pair - y)
        for j in range(GROUP):

            @pl.when(hop == j)
            def _(j=j, columns=columns):
                outs[j][:, 0:PAIR] = k[0, :, columns]
                outs[j][:, PAIR : 2 * PAIR] = v[0, :, columns]
                outs[j][:, 2 * PAIR : 3 * PAIR] = q[0, :, columns]


def pack_edges(pos, *refs):
    parts, (low, high) = refs[:GROUP], refs[GROUP:]
    y = pos[0]
    for hop in range(GROUP):
        shard = wrap(y - hop)

        @pl.when(shard < 2)
        def _(hop=hop, shard=shard):
            low[rows_at(shard * ROWS, ROWS), :] = parts[hop][:, 0 : 2 * PAIR]

        @pl.when(shard >= 2)
        def _(hop=hop, shard=shard):
            high[rows_at((shard - 2) * ROWS, ROWS), :] = parts[hop][:, 0 : 2 * PAIR]


def tile_mask(lengths, first_query, frames):
    query = first_query + lax.broadcasted_iota(jnp.int32, (TILE, 1), 0)
    low = jnp.maximum(query - REACH, 0)
    high = jnp.minimum(query + REACH, frames - 1)
    end = 0
    for recording in range(3):
        end = end + lengths[0, recording]
        low = jnp.maximum(low, jnp.where(query >= end, end, 0))
        high = jnp.minimum(high, jnp.where(query < end, end - 1, frames - 1))
    key = first_query - REACH + lax.broadcasted_iota(jnp.int32, (1, WINDOW), 1)
    return (key >= low) & (key <= high)


def head_columns(head):
    lane = lax.broadcasted_iota(jnp.int32, (1, PAIR), 1)
    return (lane >= head * HEAD_DIM) & (lane < (head + 1) * HEAD_DIM)


def forward(frames, pos, lengths, *refs):
    parts = refs[:GROUP]
    before, after = refs[GROUP : GROUP + 2]
    outs = refs[GROUP + 2 : 2 * GROUP + 2]
    q_all, k_all, v_all, context, log_total = refs[2 * GROUP + 2 :]
    y, z = pos[0], pos[1]
    k_all[0:REACH, :] = before[:, 0:PAIR]
    v_all[0:REACH, :] = before[:, PAIR : 2 * PAIR]
    k_all[REACH + OWN : SPAN, :] = after[:, 0:PAIR]
    v_all[REACH + OWN : SPAN, :] = after[:, PAIR : 2 * PAIR]
    for hop in range(GROUP):
        start = wrap(y - hop) * ROWS
        k_all[rows_at(REACH + start, ROWS), :] = parts[hop][:, 0:PAIR]
        v_all[rows_at(REACH + start, ROWS), :] = parts[hop][:, PAIR : 2 * PAIR]
        q_all[rows_at(start, ROWS), :] = parts[hop][:, 2 * PAIR : 3 * PAIR]

    def step(tile, _):
        first = pl.multiple_of(tile * TILE, TILE)
        mask = tile_mask(lengths, z * OWN + first, frames)
        query = q_all[pl.ds(first, TILE), :]
        keys = k_all[pl.ds(first, WINDOW), :]
        values = v_all[pl.ds(first, WINDOW), :]
        lane = lax.broadcasted_iota(jnp.int32, (TILE, 128), 1)
        total = jnp.zeros((TILE, PAIR), F32)
        logs = jnp.zeros((TILE, 128), F32)
        for head in range(2):
            inside = head_columns(head)
            scores = dot_nt(jnp.where(inside, query, 0), keys)
            scores = jnp.where(mask, scores, NEG_FILL)
            largest = jnp.max(scores, axis=1, keepdims=True)
            expo = jnp.exp2((scores - largest) * (SCALE * LOG2E))
            sums = jnp.sum(expo, axis=1, keepdims=True)
            product = dot(expo.astype(BF16), values) / sums
            total = jnp.where(inside, product, total)
            logs = jnp.where(lane == head, largest + jnp.log(sums) * (1.0 / SCALE), logs)
        context[pl.ds(first, TILE), :] = total.astype(BF16)
        log_total[pl.ds(first, TILE), :] = logs
        return 0

    lax.fori_loop(0, OWN // TILE, step, 0)
    for hop in range(GROUP):
        outs[hop][...] = context[rows_at(wrap(y + hop) * ROWS, ROWS), :]


def backward(frames, pos, lengths, *refs):
    parts = refs[:GROUP]
    q_all, k_all, v_all, context, log_total = refs[GROUP : GROUP + 5]
    dq, own, low, high = refs[GROUP + 5 : GROUP + 9]
    dcontext, dk, dv = refs[GROUP + 9 :]
    y, z = pos[0], pos[1]
    for hop in range(GROUP):
        dcontext[rows_at(wrap(y - hop) * ROWS, ROWS), :] = parts[hop][...]
    dk[...] = jnp.zeros_like(dk)
    dv[...] = jnp.zeros_like(dv)

    def step(tile, _):
        first = pl.multiple_of(tile * TILE, TILE)
        mask = tile_mask(lengths, z * OWN + first, frames)
        query = q_all[pl.ds(first, TILE), :]
        keys = k_all[pl.ds(first, WINDOW), :]
        values = v_all[pl.ds(first, WINDOW), :]
        grads = dcontext[pl.ds(first, TILE), :]
        product = grads.astype(F32) * context[pl.ds(first, TILE), :].astype(F32)
        logs = log_total[pl.ds(first, TILE), :]
        query_t = query.T
        grads_t = grads.T
        total = jnp.zeros((TILE, PAIR), F32)
        for head in range(2):
            inside = head_columns(head)
            own_rows = slice(head * HEAD_DIM, (head + 1) * HEAD_DIM)
            delta = jnp.sum(jnp.where(inside, product, 0.0), axis=1, keepdims=True)
            scores = dot_nt(jnp.where(inside, query, 0), keys)
            scores = jnp.where(mask, scores, NEG_FILL)
            probability = jnp.exp2((scores - logs[:, head : head + 1]) * (SCALE * LOG2E))
            gap = dot_nt(jnp.where(inside, grads, 0), values) - delta
            score_grad = (probability * gap).astype(BF16)
            total = jnp.where(inside, dot(score_grad, keys), total)
            dk[own_rows, pl.ds(first, WINDOW)] += dot(query_t[own_rows, :], score_grad)
            dv[own_rows, pl.ds(first, WINDOW)] += dot(
                grads_t[own_rows, :], probability.astype(BF16)
            )
        dq[pl.ds(first, TILE), :] = (total * SCALE).astype(BF16)
        return 0

    lax.fori_loop(0, OWN // TILE, step, 0)
    low[:, 0:PAIR] = (dk[:, 0:REACH].T * SCALE).astype(BF16)
    low[:, PAIR : 2 * PAIR] = dv[:, 0:REACH].T.astype(BF16)
    high[:, 0:PAIR] = (dk[:, REACH + OWN : SPAN].T * SCALE).astype(BF16)
    high[:, PAIR : 2 * PAIR] = dv[:, REACH + OWN : SPAN].T.astype(BF16)
    own[:, 0:PAIR] = dk[:, REACH : REACH + OWN].T * SCALE
    own[:, PAIR : 2 * PAIR] = dv[:, REACH : REACH + OWN].T


def pack_grads(pos, dq, own, from_before, from_after, *refs):
    outs, total = refs[:GROUP], refs[GROUP]
    y = pos[0]
    total[0:REACH, :] = own[0:REACH, :] + from_before[...].astype(F32)
    total[REACH:OWN, :] = own[REACH:OWN, :] + from_after[...].astype(F32)
    for hop in range(GROUP):
        rows = rows_at(wrap(y + hop) * ROWS, ROWS)
        outs[hop][:, 0 : 2 * PAIR] = total[rows, :].astype(BF16)
        outs[hop][:, 2 * PAIR : 3 * PAIR] = dq[rows, :]


def unpack_grads(pos, *refs):
    parts, (dq, dk, dv) = refs[:GROUP], refs[GROUP:]
    y = pos[0]
    for hop in range(GROUP):
        shard = wrap(y - hop)
        for head_pair in range(GROUP):

            @pl.when(shard == head_pair)
            def _(hop=hop, head_pair=head_pair):
                columns = slice(head_pair * PAIR, (head_pair + 1) * PAIR)
                dk[0, :, columns] = parts[hop][:, 0:PAIR]
                dv[0, :, columns] = parts[hop][:, PAIR : 2 * PAIR]
                dq[0, :, columns] = parts[hop][:, 2 * PAIR : 3 * PAIR]


def context_grad(pos, cot, mine, other, *refs):
    outs, weight = refs[:GROUP], refs[GROUP]
    y, x, y_low, core = pos[0], pos[2], pos[3], pos[4]
    for j in range(4):
        for t in range(2):
            for flip, source in ((0, mine), (1, other)):
                strip = wrap(x - j) * 4 + (y_low + t) % 2 * 2 + (core + flip) % 2
                start = j * 2 * STRIP + t * STRIP
                weight[rows_at(strip * STRIP, STRIP), :] = source[start : start + STRIP, :]
    for hop in range(GROUP):
        rows = rows_at(wrap(y + hop) * PAIR, PAIR)
        outs[hop][...] = dot_nt(cot[0], weight[rows, :]).astype(BF16)


def weight_term(pos, cot, *refs):
    parts, (keep, send, term) = refs[:GROUP], refs[GROUP:]
    y, x, y_low, core = pos[0], pos[2], pos[3], pos[4]
    for hop in range(GROUP):
        shard = wrap(y - hop)
        term[...] = dot(parts[hop][...].T, cot[0]).astype(BF16)
        for i in range(4):
            start = wrap(shard - x) * 2 * STRIP + (y_low + i // 2) % 2 * STRIP
            rows = rows_at(start, STRIP)
            value = term[i * STRIP : (i + 1) * STRIP, :]

            @pl.when(core == i % 2)
            def _(rows=rows, value=value):
                keep[rows, :] = value

            @pl.when(core != i % 2)
            def _(rows=rows, value=value):
                send[rows, :] = value


def project(pos, weight, *refs):
    parts, attended = refs[:GROUP], refs[GROUP]
    y = pos[0]
    for block in range(3):
        columns = slice(block * 512, (block + 1) * 512)
        total = jnp.zeros((ROWS, 512), F32)
        for hop in range(GROUP):
            rows = rows_at(wrap(y - hop) * PAIR, PAIR)
            total = total + dot(parts[hop][...], weight[rows, columns])
        attended[0, :, columns] = total.astype(BF16)


def add_cores(keep, received, *outs):
    for j in range(4):
        rows = slice(j * 2 * STRIP, (j + 1) * 2 * STRIP)
        outs[j][...] = (keep[rows, :].astype(F32) + received[rows, :].astype(F32)).astype(BF16)


def add_x(a, b, c, d, keep, send):
    total = a[...].astype(F32) + b[...].astype(F32) + c[...].astype(F32) + d[...].astype(F32)
    keep[...] = total[0:STRIP, :]
    send[...] = total[STRIP : 2 * STRIP, :].astype(BF16)


def add_y_low(keep, received, out):
    total = (keep[...] + received[...].astype(F32)).astype(BF16)
    for j in range(out.shape[0]):
        out[j, :, :] = total[:, j * PAIR : (j + 1) * PAIR]


def add_z(parts, out):
    total = parts[0].astype(F32)
    for j in range(1, parts.shape[0]):
        total = total + parts[j].astype(F32)
    total = total.astype(BF16)
    for j in range(GROUP):
        out[j, :, :] = total[:, j * STRIP : (j + 1) * STRIP]


def add_y(parts, out):
    total = parts[0].astype(F32)
    for j in range(1, GROUP):
        total = total + parts[j].astype(F32)
    out[...] = total


def on_device(queries, keys, values, rec_lengths, out_weight, cotangent):
    n_seq = lax.axis_size("seq")
    n_z = n_seq // GROUP
    frames = n_seq * ROWS
    seq_index = lax.axis_index("seq")
    strip_index = lax.axis_index("fsdp")
    pos = jnp.stack(
        [
            seq_index % GROUP,
            seq_index // GROUP,
            strip_index // 4,
            strip_index // 2 % 2,
            strip_index % 2,
        ]
    ).astype(jnp.int32)

    def along_y(block, hop):
        route = [(i, i // GROUP * GROUP + (i + hop) % GROUP) for i in range(n_seq)]
        return lax.ppermute(block, "seq", route)

    def along_z(block, hop):
        moved = hop * GROUP
        route = [(i, i + moved) for i in range(n_seq) if 0 <= i + moved < n_seq]
        return lax.ppermute(block, "seq", route)

    def along_x(block, hop):
        return lax.ppermute(block, "fsdp", [(i, (i + 4 * hop) % 16) for i in range(16)])

    def swap_y_low(block):
        return lax.ppermute(block, "fsdp", [(i, i ^ 2) for i in range(16)])

    def swap_core(block):
        return lax.ppermute(block, "fsdp", [(i, i ^ 1) for i in range(16)])

    def exchange(chunks):
        return [chunks[0]] + [along_y(chunks[hop], hop) for hop in range(1, GROUP)]

    chunk = struct((ROWS, 3 * PAIR))
    packed = call(pack_heads, (chunk,) * GROUP, (pos, queries, keys, values))
    parts = exchange(packed)
    strips = jnp.concatenate([out_weight, swap_y_low(out_weight)], axis=0)
    mine = jnp.concatenate([strips] + [along_x(strips, hop) for hop in (1, 2, 3)], axis=0)
    other = swap_core(mine)

    edge = struct((REACH, 2 * PAIR))
    low, high = call(pack_edges, (edge, edge), (pos, *parts))
    after, before = along_z(low, -1), along_z(high, 1)

    square = struct((ROWS, PAIR))
    *grads, weight = call(
        context_grad,
        (square,) * GROUP + (struct((INNER, WIDTH)),),
        (pos, cotangent, mine, other),
        flops=2 * ROWS * INNER * WIDTH,
    )
    pair_flops = 2 * 2 * OWN * WINDOW * PAIR
    *context_parts, q_all, k_all, v_all, context, log_total = call(
        lambda *refs: forward(frames, *refs),
        (square,) * GROUP
        + (
            struct((OWN, PAIR)),
            struct((SPAN, PAIR)),
            struct((SPAN, PAIR)),
            struct((OWN, PAIR)),
            struct((OWN, 128), F32),
        ),
        (pos, rec_lengths, *parts, before, after),
        flops=2 * pair_flops,
        smem=2,
    )
    grads = exchange(grads)
    context_parts = exchange(context_parts)

    half = struct((INNER // 2, WIDTH))
    keep, send = call(
        weight_term,
        (half, half),
        (pos, cotangent, *context_parts),
        flops=2 * ROWS * INNER * WIDTH,
        scratch=[pltpu.VMEM((PAIR, WIDTH), BF16)],
    )
    received = swap_core(send)

    dq, own, low, high = call(
        lambda *refs: backward(frames, *refs),
        (struct((OWN, PAIR)), struct((OWN, 2 * PAIR), F32), edge, edge),
        (pos, rec_lengths, *grads, q_all, k_all, v_all, context, log_total),
        flops=5 * pair_flops,
        scratch=[
            pltpu.VMEM((OWN, PAIR), BF16),
            pltpu.VMEM((PAIR, SPAN), F32),
            pltpu.VMEM((PAIR, SPAN), F32),
        ],
        smem=2,
    )
    from_after, from_before = along_z(low, -1), along_z(high, 1)

    sums = call(add_cores, (struct((2 * STRIP, WIDTH)),) * 4, (keep, received), smem=0)
    sums = [sums[0]] + [along_x(sums[hop], hop) for hop in (1, 2, 3)]
    keep, send = call(
        add_x, (struct((STRIP, WIDTH), F32), struct((STRIP, WIDTH))), tuple(sums), smem=0
    )
    received = swap_y_low(send)

    attended = call(
        project,
        struct((1, ROWS, WIDTH)),
        (pos, weight, *context_parts),
        flops=2 * ROWS * INNER * WIDTH,
    )

    outs = call(
        pack_grads,
        (chunk,) * GROUP,
        (pos, dq, own, from_before, from_after),
        scratch=[pltpu.VMEM((OWN, 2 * PAIR), F32)],
    )
    outs = exchange(outs)
    full = struct((1, ROWS, INNER))
    grad_queries, grad_keys, grad_values = call(unpack_grads, (full, full, full), (pos, *outs))

    z_groups = [[z * GROUP + y for z in range(n_z)] for y in range(GROUP)]
    y_groups = [[z * GROUP + y for y in range(GROUP)] for z in range(n_z)]
    blocks = call(add_y_low, struct((n_z, STRIP, PAIR)), (keep, received), smem=0)
    blocks = lax.all_to_all(blocks, "seq", 0, 0, axis_index_groups=z_groups)
    blocks = call(add_z, struct((GROUP, STRIP, STRIP)), (blocks,), smem=0)
    blocks = lax.all_to_all(blocks, "seq", 0, 0, axis_index_groups=y_groups)
    grad_weight = call(add_y, struct((STRIP, STRIP), F32), (blocks,), smem=0)
    return attended, grad_queries, grad_keys, grad_values, grad_weight


def solution(mesh):
    rows = P("fsdp", "seq", None)
    return jax.shard_map(
        on_device,
        mesh=mesh,
        in_specs=(rows, rows, rows, P("fsdp", None), P("fsdp", None), rows),
        out_specs=(rows, rows, rows, rows, P("fsdp", "seq")),
        check_vma=False,
    )
```

time: 544 us -> 186 us (0.34); the launches traced: 535 us -> 184 us
  matrix products: 213 us -> 0 us
  waiting for transfers between devices: 157 us -> 32.1 us
  starting transfers between devices: 35.5 us -> 111 us
  local copies, waits for them, and re-layouts: 85.7 us -> 12.8 us
  Pallas kernels: 0 us -> 26.9 us
  other arithmetic: 25.4 us -> 0 us
  between operations: 16.2 us -> 1.28 us
    dot_general x219 -> x0, matrix products: 213 us -> none  [the longest x40 64.6 us: head_backward(): jnp.dot(score_grad, key_head, preferred_element_type=jnp.float32) * scale]
    reduce_scatter x1 -> x0, waiting for transfers between devices: 69.4 us -> none  [on_device(): lax.psum_scatter(term.astype(jnp.bfloat16), 'seq', scatter_dimension=1, t...]
    ppermute x8 -> x26, starting transfers between devices: 35.2 us -> 98.6 us  [the longest x12 53.3 us: along_y(): return lax.ppermute(block, 'seq', route)]
    unnamed x4 -> x0, waiting for transfers between devices: 61.4 us -> none
    pallas_call x0 -> x14, Pallas kernels: none -> 26.9 us  [call(): pl.pallas_call(body, out_shape=out_shape, in_specs=[scalars] * smem + [vm...]
    reshape x21 -> x0, local copies, waits for them, and re-layouts: 20.4 us -> none  [the longest x10 16 us: merge_heads(): stacked.transpose(1, 0, 2).reshape(stacked.shape[1], HEADS * HEAD_DIM)]
    transpose x10 -> x0, local copies, waits for them, and re-layouts: 13.4 us -> none  [merge_heads(): stacked.transpose(1, 0, 2).reshape(stacked.shape[1], HEADS * HEAD_DIM)]
    all_to_all x0 -> x2, starting transfers between devices: none -> 12.7 us  [the longest x1 9.4 us: on_device(): blocks = lax.all_to_all(blocks, 'seq', 0, 0, axis_index_groups=z_groups)]
  transfers between devices with their start and end apart: 11 -> 28, of which waited for: 6 -> 7; matrix products, arithmetic and copies ran while one was open for 60% -> 1% of each run, Pallas kernels for 0% -> 14%
where the time goes in v1:
time: 186 us; the launch traced here: 184 us
  starting transfers between devices  111 us (60%)
  waiting for transfers between devices  32.1 us (17%)
  Pallas kernels  26.9 us (14%)
  local copies, waits for them, and re-layouts  12.8 us (7%)
    ppermute x12, starting transfers between devices, along_y(): return lax.ppermute(block, 'seq', route)  53.3 us
    pallas_call x14, Pallas kernels, call(): pl.pallas_call(body, out_shape=out_shape, in_specs=[scalars] * smem + [vm...  26.9 us
    ppermute x6, starting transfers between devices, along_x(): lax.ppermute(block, 'fsdp', [(i, (i + 4 * hop) % 16) for i in range(16)])  21.7 us
    ppermute x12, waiting for transfers between devices, along_y(): return lax.ppermute(block, 'seq', route)  17.1 us
    unnamed x53, local copies, waits for them, and re-layouts  12.7 us
    ppermute x4, starting transfers between devices, along_z(): return lax.ppermute(block, 'seq', route)  11.3 us
    all_to_all x1, starting transfers between devices, on_device(): blocks = lax.all_to_all(blocks, 'seq', 0, 0, axis_index_groups=z_groups)  9.4 us
    ppermute x4, waiting for transfers between devices, along_z(): return lax.ppermute(block, 'seq', route)  9.22 us
  transfers between devices with their start and end apart: 28, of which 7 were waited for; matrix products, arithmetic and copies ran while one was open for 1% of the time, Pallas kernels for 14%

profile of v1, /device:TPU:1, one launch (start us, length us, event | category | flops | bytes accessed | tf_op | source)
XLA Modules:
  0.0 184.4 jit_solution(14835264201317160339)
XLA Ops:
  0.7 4.2 %collective-permute-start = (bf16[48,1536]{1,0:T(8,128)(2,1)}, bf16[48,1536]{1,0:T(8,128)(2,1)S(1)}, u32[]{:S(2)}, u32[]{:S(2)}) collective-permute-start(bf16[48,1536]{1,0:T(8,128)(2,1)} %param.10), channel_id=1, source_target_pairs={{0,2},{1,3},{2,0},{3,1},{4,6},{5,7},{6,4},{7,5},{8,10},{9,11},{10,... | collective-permute-start | bytes 442376 | tf_op jit(solution)/shard_map/ppermute | solution.py:338
  7.6 4.0 %collective-permute-start.1 = (bf16[96,1536]{1,0:T(8,128)(2,1)S(1)}, bf16[96,1536]{1,0:T(8,128)(2,1)S(1)}, u32[]{:S(2)}, u32[]{:S(2)}) collective-permute-start(bf16[96,1536]{1,0:T(8,128)(2,1)S(1)} %get-tuple-element.83), channel_id=1, source_target_pairs={{0,4},{1,5},{2,6},{3,7},{4,8},{5,9},{6,10},{7,11},{8,12},{9,13},{1... | collective-permute-start | bytes 884744 | tf_op jit(solution)/shard_map/ppermute | solution.py:335
  12.8 4.2 %collective-permute-start.5 = (bf16[192,576]{1,0:T(8,128)(2,1)S(1)}, bf16[192,576]{1,0:T(8,128)(2,1)S(1)}, u32[]{:S(2)}, u32[]{:S(2)}) collective-permute-start(bf16[192,576]{1,0:T(8,128)(2,1)S(1)} %get-tuple-element.46), channel_id=1, source_target_pairs={{0,16},{16,32},{32,48},{48,0},{64,80},{80,96},{96,112},{112,64},{1... | collective-permute-start | bytes 663560 | tf_op jit(solution)/shard_map/ppermute | solution.py:327
  17.0 5.7 %collective-permute-start.6 = (bf16[192,576]{1,0:T(8,128)(2,1)S(1)}, bf16[192,576]{1,0:T(8,128)(2,1)S(1)}, u32[]{:S(2)}, u32[]{:S(2)}) collective-permute-start(bf16[192,576]{1,0:T(8,128)(2,1)S(1)} %get-tuple-element.47), channel_id=1, source_target_pairs={{0,32},{16,48},{32,0},{48,16},{64,96},{80,112},{96,64},{112,80},{1... | collective-permute-start | bytes 663560 | tf_op jit(solution)/shard_map/ppermute | solution.py:327
  22.7 5.0 %collective-permute-start.7 = (bf16[192,576]{1,0:T(8,128)(2,1)S(1)}, bf16[192,576]{1,0:T(8,128)(2,1)S(1)}, u32[]{:S(2)}, u32[]{:S(2)}) collective-permute-start(bf16[192,576]{1,0:T(8,128)(2,1)S(1)} %get-tuple-element.48), channel_id=1, source_target_pairs={{0,48},{16,0},{32,16},{48,32},{64,112},{80,64},{96,80},{112,96},{1... | collective-permute-start | bytes 663560 | tf_op jit(solution)/shard_map/ppermute | solution.py:327
  27.7 4.4 %collective-permute-start.2 = (bf16[96,1536]{1,0:T(8,128)(2,1)S(1)}, bf16[96,1536]{1,0:T(8,128)(2,1)S(1)}, u32[]{:S(2)}, u32[]{:S(2)}) collective-permute-start(bf16[96,1536]{1,0:T(8,128)(2,1)S(1)} %get-tuple-element.83), channel_id=1, source_target_pairs={{0,8},{1,9},{2,10},{3,11},{4,12},{5,13},{6,14},{7,15},{8,0},{9,1},... | collective-permute-start | bytes 884744 | tf_op jit(solution)/shard_map/ppermute | solution.py:335
  32.0 3.1 %collective-permute-start.3 = (bf16[96,1536]{1,0:T(8,128)(2,1)S(1)}, bf16[96,1536]{1,0:T(8,128)(2,1)S(1)}, u32[]{:S(2)}, u32[]{:S(2)}) collective-permute-start(bf16[96,1536]{1,0:T(8,128)(2,1)S(1)} %get-tuple-element.83), channel_id=1, source_target_pairs={{0,12},{1,13},{2,14},{3,15},{4,0},{5,1},{6,2},{7,3},{8,4},{9,5},{1... | collective-permute-start | bytes 884744 | tf_op jit(solution)/shard_map/ppermute | solution.py:335
  36.1 9.4 %collective-permute-done.7.refs_3_.refs_5_ = bf16[192,576]{1,0:T(8,128)(2,1)S(1)} collective-permute-done((bf16[192,576]{1,0:T(8,128)(2,1)S(1)}, bf16[192,576]{1,0:T(8,128)(2,1)S(1)}, u32[]{:S(2)}, u32[]{:S(2)}) %collective-permute-start.7) | collective-permute-done | bytes 221216 | tf_op jit(solution)/shard_map/ppermute | solution.py:327
  46.2 4.0 %collective-permute-start.8 = (bf16[384,384]{1,0:T(8,128)(2,1)S(1)}, bf16[384,384]{1,0:T(8,128)(2,1)S(1)}, u32[]{:S(2)}, u32[]{:S(2)}) collective-permute-start(bf16[384,384]{1,0:T(8,128)(2,1)S(1)} %get-tuple-element.49), channel_id=1, source_target_pairs={{0,64},{16,80},{32,96},{48,112},{64,128},{80,144},{96,160},{112,17... | collective-permute-start | bytes 884744 | tf_op jit(solution)/shard_map/ppermute | solution.py:332
  51.6 4.5 %collective-permute-done.8.refs_6_ = bf16[384,384]{1,0:T(8,128)(2,1)S(1)} collective-permute-done((bf16[384,384]{1,0:T(8,128)(2,1)S(1)}, bf16[384,384]{1,0:T(8,128)(2,1)S(1)}, u32[]{:S(2)}, u32[]{:S(2)}) %collective-permute-start.8) | collective-permute-done | bytes 294944 | tf_op jit(solution)/shard_map/ppermute | solution.py:332
  56.0 4.8 %collective-permute-done.9.refs_7_ = bf16[384,384]{1,0:T(8,128)(2,1)S(1)} collective-permute-done((bf16[384,384]{1,0:T(8,128)(2,1)S(1)}, bf16[384,384]{1,0:T(8,128)(2,1)S(1)}, u32[]{:S(2)}, u32[]{:S(2)}) %collective-permute-start.9) | collective-permute-done | bytes 294944 | tf_op jit(solution)/shard_map/ppermute | solution.py:332
  60.8 5.2 %shard_map.104 = (bf16[192,192]{1,0:T(8,128)(2,1)S(1)}, bf16[192,192]{1,0:T(8,128)(2,1)S(1)}, bf16[192,192]{1,0:T(8,128)(2,1)S(1)}, bf16[192,192]{1,0:T(8,128)(2...) custom-call(s32[5]{0:T(128)S(1)} %stack.23.pos.refs_0_, ...), custom_call_target="tpu_custom_call" | custom-call | flops 1207959552 | bytes 3932196 | tf_op jit(solution)/shard_map/pallas_call | solution.py:36
  66.0 4.2 %collective-permute-start.10 = (bf16[192,192]{1,0:T(8,128)(2,1)S(1)}, bf16[192,192]{1,0:T(8,128)(2,1)S(1)}, u32[]{:S(2)}, u32[]{:S(2)}) collective-permute-start(bf16[192,192]{1,0:T(8,128)(2,1)S(1)} %get-tuple-element.52), channel_id=1, source_target_pairs={{0,16},{16,32},{32,48},{48,0},{64,80},{80,96},{96,112},{112,64},{1... | collective-permute-start | bytes 221192 | tf_op jit(solution)/shard_map/ppermute | solution.py:327
  70.2 4.8 %collective-permute-start.11 = (bf16[192,192]{1,0:T(8,128)(2,1)S(1)}, bf16[192,192]{1,0:T(8,128)(2,1)S(1)}, u32[]{:S(2)}, u32[]{:S(2)}) collective-permute-start(bf16[192,192]{1,0:T(8,128)(2,1)S(1)} %get-tuple-element.53), channel_id=1, source_target_pairs={{0,32},{16,48},{32,0},{48,16},{64,96},{80,112},{96,64},{112,80},{1... | collective-permute-start | bytes 221192 | tf_op jit(solution)/shard_map/ppermute | solution.py:327
  75.0 4.9 %collective-permute-start.12 = (bf16[192,192]{1,0:T(8,128)(2,1)S(1)}, bf16[192,192]{1,0:T(8,128)(2,1)S(1)}, u32[]{:S(2)}, u32[]{:S(2)}) collective-permute-start(bf16[192,192]{1,0:T(8,128)(2,1)S(1)} %get-tuple-element.54), channel_id=1, source_target_pairs={{0,48},{16,0},{32,16},{48,32},{64,112},{80,64},{96,80},{112,96},{1... | collective-permute-start | bytes 221192 | tf_op jit(solution)/shard_map/ppermute | solution.py:327
  80.0 4.1 %collective-permute-start.4 = (bf16[384,1536]{1,0:T(8,128)(2,1)S(1)}, bf16[384,1536]{1,0:T(8,128)(2,1)S(1)}, u32[]{:S(2)}, u32[]{:S(2)}) collective-permute-start(bf16[384,1536]{1,0:T(8,128)(2,1)S(1)} %constant_dynamic-update-slice_fusion.2.mine), channel_id=1, source_target_pairs={{0,1},{1,0},{2,3},{3,2},{4,5},{5,4},{6,7},{7,6},{8,9},{9,8},{10,11... | collective-permute-start | bytes 3538952 | tf_op jit(solution)/shard_map/ppermute | solution.py:341
  84.1 2.1 %shard_map.109 = (bf16[384,1536]{1,0:T(8,128)(2,1)S(1)}, bf16[384,1536]{1,0:T(8,128)(2,1)S(1)}) custom-call(s32[5]{0:T(128)S(1)} %stack.23.pos.refs_0_, bf16[1,192,1536]{2,1,0:T(8,128)(2,1)S(1)} %copy-done.1, bf16[192,192]{1,0:T(8,128)(2,1)S(1)} %get-tuple-element.51.refs_0_, bf16[192,192]{1,0:T(8,128)(2,1)S(1)} %collective-permute-done.10.refs_1_, ...), custom_call_target="tpu_custom_call" | custom-call | flops 452984832 | bytes 3244052 | tf_op jit(solution)/shard_map/pallas_call | solution.py:36
  89.9 3.6 %collective-permute-start.13 = (bf16[192,192]{1,0:T(8,128)(2,1)S(1)}, bf16[192,192]{1,0:T(8,128)(2,1)S(1)}, u32[]{:S(2)}, u32[]{:S(2)}) collective-permute-start(bf16[192,192]{1,0:T(8,128)(2,1)S(1)} %get-tuple-element.56), channel_id=1, source_target_pairs={{0,16},{16,32},{32,48},{48,0},{64,80},{80,96},{96,112},{112,64},{1... | collective-permute-start | bytes 221192 | tf_op jit(solution)/shard_map/ppermute | solution.py:327
  93.5 6.5 %collective-permute-start.14 = (bf16[192,192]{1,0:T(8,128)(2,1)S(1)}, bf16[192,192]{1,0:T(8,128)(2,1)S(1)}, u32[]{:S(2)}, u32[]{:S(2)}) collective-permute-start(bf16[192,192]{1,0:T(8,128)(2,1)S(1)} %get-tuple-element.57), channel_id=1, source_target_pairs={{0,32},{16,48},{32,0},{48,16},{64,96},{80,112},{96,64},{112,80},{1... | collective-permute-start | bytes 221192 | tf_op jit(solution)/shard_map/ppermute | solution.py:327
  102.2 3.1 %collective-permute-start.22 = (bf16[96,1536]{1,0:T(8,128)(2,1)S(1)}, bf16[96,1536]{1,0:T(8,128)(2,1)S(1)}, u32[]{:S(2)}, u32[]{:S(2)}) collective-permute-start(bf16[96,1536]{1,0:T(8,128)(2,1)S(1)} %get-tuple-element.78), channel_id=1, source_target_pairs={{0,4},{1,5},{2,6},{3,7},{4,8},{5,9},{6,10},{7,11},{8,12},{9,13},{1... | collective-permute-start | bytes 884744 | tf_op jit(solution)/shard_map/ppermute | solution.py:335
  105.4 3.4 %collective-permute-start.23 = (bf16[96,1536]{1,0:T(8,128)(2,1)S(1)}, bf16[96,1536]{1,0:T(8,128)(2,1)S(1)}, u32[]{:S(2)}, u32[]{:S(2)}) collective-permute-start(bf16[96,1536]{1,0:T(8,128)(2,1)S(1)} %get-tuple-element.79), channel_id=1, source_target_pairs={{0,8},{1,9},{2,10},{3,11},{4,12},{5,13},{6,14},{7,15},{8,0},{9,1},... | collective-permute-start | bytes 884744 | tf_op jit(solution)/shard_map/ppermute | solution.py:335
  108.7 3.8 %collective-permute-start.24 = (bf16[96,1536]{1,0:T(8,128)(2,1)S(1)}, bf16[96,1536]{1,0:T(8,128)(2,1)S(1)}, u32[]{:S(2)}, u32[]{:S(2)}) collective-permute-start(bf16[96,1536]{1,0:T(8,128)(2,1)S(1)} %get-tuple-element.80), channel_id=1, source_target_pairs={{0,12},{1,13},{2,14},{3,15},{4,0},{5,1},{6,2},{7,3},{8,4},{9,5},{1... | collective-permute-start | bytes 884744 | tf_op jit(solution)/shard_map/ppermute | solution.py:335
  112.5 8.1 %shard_map.106 = (bf16[768,192]{1,0:T(8,128)(2,1)S(1)}, f32[768,384]{1,0:T(8,128)S(1)}, bf16[384,384]{1,0:T(8,128)(2,1)}, bf16[384,384]{1,0:T(8,128)(2,1)}) custom-call(s32[5]{0:T(128)S(1)} %stack.23.pos.refs_0_, s32[1,4]{1,0:T(1,128)S(1)} %copy-done.23, bf16[192,192]{1,0:T(8,128)(2,1)S(1)} %get-tuple-element.55.refs_2_, ...), custom_call_target="tpu_custom_call" | custom-call | flops 3019898880 | bytes 4522020 | tf_op jit(solution)/shard_map/pallas_call | solution.py:36
  120.6 4.7 %collective-permute-start.16 = (bf16[384,384]{1,0:T(8,128)(2,1)}, bf16[384,384]{1,0:T(8,128)(2,1)}, u32[]{:S(2)}, u32[]{:S(2)}) collective-permute-start(bf16[384,384]{1,0:T(8,128)(2,1)} %get-tuple-element.66), channel_id=1, source_target_pairs={{0,64},{16,80},{32,96},{48,112},{64,128},{80,144},{96,160},{112,17... | collective-permute-start | bytes 884744 | tf_op jit(solution)/shard_map/ppermute | solution.py:332
  128.7 4.0 %collective-permute-done.25.received = bf16[48,1536]{1,0:T(8,128)(2,1)S(1)} collective-permute-done((bf16[48,1536]{1,0:T(8,128)(2,1)S(1)}, bf16[48,1536]{1,0:T(8,128)(2,1)S(1)}, u32[]{:S(2)}, u32[]{:S(2)}) %collective-permute-start.25) | collective-permute-done | bytes 147488 | tf_op jit(solution)/shard_map/ppermute | solution.py:338
  133.5 9.4 %all-to-all-start = ((bf16[8,48,192]{2,1,0:T(8,128)(2,1)}), bf16[8,48,192]{2,1,0:T(8,128)(2,1)}, u32[]{:S(2)}, u32[]{:S(2)}) async-start(bf16[8,48,192]{2,1,0:T(8,128)(2,1)} %copy-done), calls=%async_computation | async-start | bytes 393216 | tf_op jit(solution)/shard_map/all_to_all | solution.py:433
  146.7 4.3 %collective-permute-start.18 = (bf16[192,576]{1,0:T(8,128)(2,1)}, bf16[192,576]{1,0:T(8,128)(2,1)S(1)}, u32[]{:S(2)}, u32[]{:S(2)}) collective-permute-start(bf16[192,576]{1,0:T(8,128)(2,1)} %get-tuple-element.69), channel_id=1, source_target_pairs={{0,16},{16,32},{32,48},{48,0},{64,80},{80,96},{96,112},{112,64},{1... | collective-permute-start | bytes 663560 | tf_op jit(solution)/shard_map/ppermute | solution.py:327
  151.0 2.8 %collective-permute-start.19 = (bf16[192,576]{1,0:T(8,128)(2,1)}, bf16[192,576]{1,0:T(8,128)(2,1)S(1)}, u32[]{:S(2)}, u32[]{:S(2)}) collective-permute-start(bf16[192,576]{1,0:T(8,128)(2,1)} %get-tuple-element.70), channel_id=1, source_target_pairs={{0,32},{16,48},{32,0},{48,16},{64,96},{80,112},{96,64},{112,80},{1... | collective-permute-start | bytes 663560 | tf_op jit(solution)/shard_map/ppermute | solution.py:327
  153.8 5.5 %collective-permute-start.20 = (bf16[192,576]{1,0:T(8,128)(2,1)}, bf16[192,576]{1,0:T(8,128)(2,1)S(1)}, u32[]{:S(2)}, u32[]{:S(2)}) collective-permute-start(bf16[192,576]{1,0:T(8,128)(2,1)} %get-tuple-element.71), channel_id=1, source_target_pairs={{0,48},{16,0},{32,16},{48,32},{64,112},{80,64},{96,80},{112,96},{1... | collective-permute-start | bytes 663560 | tf_op jit(solution)/shard_map/ppermute | solution.py:327
  161.1 3.3 %all-to-all-start.1 = ((bf16[4,2,1152]{2,1,0:T(2,128)(2,1)}), bf16[4,2,1152]{2,1,0:T(2,128)(2,1)S(1)}, u32[]{:S(2)}, u32[]{:S(2)}) async-start(bf16[4,2,1152]{2,1,0:T(2,128)(2,1)} %reshape.10), calls=%async_computation.1 | async-start | bytes 36864 | tf_op jit(solution)/shard_map/all_to_all | solution.py:435
  168.0 2.1 %shard_map.105 = bf16[1,192,1536]{2,1,0:T(8,128)(2,1)} custom-call(s32[5]{0:T(128)S(1)} %stack.23.pos.refs_0_, bf16[768,1536]{1,0:T(8,128)(2,1)S(1)} %get-tuple-element.44.weight, bf16[192,192]{1,0:T(8,128)(2,1)S(1)} %copy-done.16, bf16[192,192]{1,0:T(8,128)(2,1)S(1)} %copy-done.18, bf16[192,192]{1,0:T(8,128)(2,1)S(1)} %copy-done.20, ...), custom_call_target="tpu_custom_call" | custom-call | flops 452984832 | bytes 3244052 | tf_op jit(solution)/shard_map/pallas_call | solution.py:36
  171.5 6.7 %collective-permute-done.20.refs_3_ = bf16[192,576]{1,0:T(8,128)(2,1)S(1)} collective-permute-done((bf16[192,576]{1,0:T(8,128)(2,1)}, bf16[192,576]{1,0:T(8,128)(2,1)S(1)}, u32[]{:S(2)}, u32[]{:S(2)}) %collective-permute-start.20) | collective-permute-done | bytes 221216 | tf_op jit(solution)/shard_map/ppermute | solution.py:327
  (94 shorter events, 33.6 us)
Async XLA Ops:
  0.7 6.9 %collective-permute-start = (bf16[48,1536]{1,0:T(8,128)(2,1)}, bf16[48,1536]{1,0:T(8,128)(2,1)S(1)}, u32[]{:S(2)}, u32[]{:S(2)}) collective-permute-start(bf16[48,1536]{1,0:T(8,128)(2,1)} %param.10), channel_id=1, source_target_pairs={{0,2},{1,3},{2,0},{3,1},{4,6},{5,7},{6,4},{7,5},{8,10},{9,11},{10,... | collective-permute-start | bytes 442376 | tf_op jit(solution)/shard_map/ppermute | solution.py:338
  7.6 43.9 %collective-permute-start.1 = (bf16[96,1536]{1,0:T(8,128)(2,1)S(1)}, bf16[96,1536]{1,0:T(8,128)(2,1)S(1)}, u32[]{:S(2)}, u32[]{:S(2)}) collective-permute-start(bf16[96,1536]{1,0:T(8,128)(2,1)S(1)} %get-tuple-element.83), channel_id=1, source_target_pairs={{0,4},{1,5},{2,6},{3,7},{4,8},{5,9},{6,10},{7,11},{8,12},{9,13},{1... | collective-permute-start | bytes 884744 | tf_op jit(solution)/shard_map/ppermute | solution.py:335
  12.8 48.0 %copy-start.23 = (s32[1,4]{1,0:T(1,128)S(1)}, s32[1,4]{1,0:T(1,128)}, u32[]{:S(2)}) copy-start(s32[1,4]{1,0:T(1,128)} %refs_1_.3) | copy-start | bytes 52
  12.8 19.2 %collective-permute-start.5 = (bf16[192,576]{1,0:T(8,128)(2,1)S(1)}, bf16[192,576]{1,0:T(8,128)(2,1)S(1)}, u32[]{:S(2)}, u32[]{:S(2)}) collective-permute-start(bf16[192,576]{1,0:T(8,128)(2,1)S(1)} %get-tuple-element.46), channel_id=1, source_target_pairs={{0,16},{16,32},{32,48},{48,0},{64,80},{80,96},{96,112},{112,64},{1... | collective-permute-start | bytes 663560 | tf_op jit(solution)/shard_map/ppermute | solution.py:327
  17.0 19.1 %collective-permute-start.6 = (bf16[192,576]{1,0:T(8,128)(2,1)S(1)}, bf16[192,576]{1,0:T(8,128)(2,1)S(1)}, u32[]{:S(2)}, u32[]{:S(2)}) collective-permute-start(bf16[192,576]{1,0:T(8,128)(2,1)S(1)} %get-tuple-element.47), channel_id=1, source_target_pairs={{0,32},{16,48},{32,0},{48,16},{64,96},{80,112},{96,64},{112,80},{1... | collective-permute-start | bytes 663560 | tf_op jit(solution)/shard_map/ppermute | solution.py:327
  22.7 22.8 %collective-permute-start.7 = (bf16[192,576]{1,0:T(8,128)(2,1)S(1)}, bf16[192,576]{1,0:T(8,128)(2,1)S(1)}, u32[]{:S(2)}, u32[]{:S(2)}) collective-permute-start(bf16[192,576]{1,0:T(8,128)(2,1)S(1)} %get-tuple-element.48), channel_id=1, source_target_pairs={{0,48},{16,0},{32,16},{48,32},{64,112},{80,64},{96,80},{112,96},{1... | collective-permute-start | bytes 663560 | tf_op jit(solution)/shard_map/ppermute | solution.py:327
  27.7 23.9 %collective-permute-start.2 = (bf16[96,1536]{1,0:T(8,128)(2,1)S(1)}, bf16[96,1536]{1,0:T(8,128)(2,1)S(1)}, u32[]{:S(2)}, u32[]{:S(2)}) collective-permute-start(bf16[96,1536]{1,0:T(8,128)(2,1)S(1)} %get-tuple-element.83), channel_id=1, source_target_pairs={{0,8},{1,9},{2,10},{3,11},{4,12},{5,13},{6,14},{7,15},{8,0},{9,1},... | collective-permute-start | bytes 884744 | tf_op jit(solution)/shard_map/ppermute | solution.py:335
  32.0 47.9 %collective-permute-start.3 = (bf16[96,1536]{1,0:T(8,128)(2,1)S(1)}, bf16[96,1536]{1,0:T(8,128)(2,1)S(1)}, u32[]{:S(2)}, u32[]{:S(2)}) collective-permute-start(bf16[96,1536]{1,0:T(8,128)(2,1)S(1)} %get-tuple-element.83), channel_id=1, source_target_pairs={{0,12},{1,13},{2,14},{3,15},{4,0},{5,1},{6,2},{7,3},{8,4},{9,5},{1... | collective-permute-start | bytes 884744 | tf_op jit(solution)/shard_map/ppermute | solution.py:335
  46.2 9.9 %collective-permute-start.8 = (bf16[384,384]{1,0:T(8,128)(2,1)S(1)}, bf16[384,384]{1,0:T(8,128)(2,1)S(1)}, u32[]{:S(2)}, u32[]{:S(2)}) collective-permute-start(bf16[384,384]{1,0:T(8,128)(2,1)S(1)} %get-tuple-element.49), channel_id=1, source_target_pairs={{0,64},{16,80},{32,96},{48,112},{64,128},{80,144},{96,160},{112,17... | collective-permute-start | bytes 884744 | tf_op jit(solution)/shard_map/ppermute | solution.py:332
  50.2 10.6 %collective-permute-start.9 = (bf16[384,384]{1,0:T(8,128)(2,1)S(1)}, bf16[384,384]{1,0:T(8,128)(2,1)S(1)}, u32[]{:S(2)}, u32[]{:S(2)}) collective-permute-start(bf16[384,384]{1,0:T(8,128)(2,1)S(1)} %get-tuple-element.50), channel_id=1, source_target_pairs={{64,0},{80,16},{96,32},{112,48},{128,64},{144,80},{160,96},{176,11... | collective-permute-start | bytes 884744 | tf_op jit(solution)/shard_map/ppermute | solution.py:332
  51.6 32.5 %copy-start.1 = (bf16[1,192,1536]{2,1,0:T(8,128)(2,1)S(1)}, bf16[1,192,1536]{2,1,0:T(8,128)(2,1)}, u32[]{:S(2)}) copy-start(bf16[1,192,1536]{2,1,0:T(8,128)(2,1)} %cot.3) | copy-start | bytes 1769476
  66.0 22.4 %copy-start.15 = (bf16[192,192]{1,0:T(8,128)(2,1)}, bf16[192,192]{1,0:T(8,128)(2,1)S(1)}, u32[]{:S(2)}) copy-start(bf16[192,192]{1,0:T(8,128)(2,1)S(1)} %get-tuple-element.51.refs_0_) | copy-start | bytes 221188
  66.0 18.1 %collective-permute-start.10 = (bf16[192,192]{1,0:T(8,128)(2,1)S(1)}, bf16[192,192]{1,0:T(8,128)(2,1)S(1)}, u32[]{:S(2)}, u32[]{:S(2)}) collective-permute-start(bf16[192,192]{1,0:T(8,128)(2,1)S(1)} %get-tuple-element.52), channel_id=1, source_target_pairs={{0,16},{16,32},{32,48},{48,0},{64,80},{80,96},{96,112},{112,64},{1... | collective-permute-start | bytes 221192 | tf_op jit(solution)/shard_map/ppermute | solution.py:327
  70.2 13.9 %collective-permute-start.11 = (bf16[192,192]{1,0:T(8,128)(2,1)S(1)}, bf16[192,192]{1,0:T(8,128)(2,1)S(1)}, u32[]{:S(2)}, u32[]{:S(2)}) collective-permute-start(bf16[192,192]{1,0:T(8,128)(2,1)S(1)} %get-tuple-element.53), channel_id=1, source_target_pairs={{0,32},{16,48},{32,0},{48,16},{64,96},{80,112},{96,64},{112,80},{1... | collective-permute-start | bytes 221192 | tf_op jit(solution)/shard_map/ppermute | solution.py:327
  75.0 9.1 %collective-permute-start.12 = (bf16[192,192]{1,0:T(8,128)(2,1)S(1)}, bf16[192,192]{1,0:T(8,128)(2,1)S(1)}, u32[]{:S(2)}, u32[]{:S(2)}) collective-permute-start(bf16[192,192]{1,0:T(8,128)(2,1)S(1)} %get-tuple-element.54), channel_id=1, source_target_pairs={{0,48},{16,0},{32,16},{48,32},{64,112},{80,64},{96,80},{112,96},{1... | collective-permute-start | bytes 221192 | tf_op jit(solution)/shard_map/ppermute | solution.py:327
  80.0 8.4 %collective-permute-start.4 = (bf16[384,1536]{1,0:T(8,128)(2,1)S(1)}, bf16[384,1536]{1,0:T(8,128)(2,1)S(1)}, u32[]{:S(2)}, u32[]{:S(2)}) collective-permute-start(bf16[384,1536]{1,0:T(8,128)(2,1)S(1)} %constant_dynamic-update-slice_fusion.2.mine), channel_id=1, source_target_pairs={{0,1},{1,0},{2,3},{3,2},{4,5},{5,4},{6,7},{7,6},{8,9},{9,8},{10,11... | collective-permute-start | bytes 3538952 | tf_op jit(solution)/shard_map/ppermute | solution.py:341
  86.3 15.7 %collective-permute-start.21 = (bf16[384,1536]{1,0:T(8,128)(2,1)S(1)}, bf16[384,1536]{1,0:T(8,128)(2,1)S(1)}, u32[]{:S(2)}, u32[]{:S(2)}) collective-permute-start(bf16[384,1536]{1,0:T(8,128)(2,1)S(1)} %get-tuple-element.76), channel_id=1, source_target_pairs={{0,1},{1,0},{2,3},{3,2},{4,5},{5,4},{6,7},{7,6},{8,9},{9,8},{10,11... | collective-permute-start | bytes 3538952 | tf_op jit(solution)/shard_map/ppermute | solution.py:341
  89.9 18.8 %collective-permute-start.13 = (bf16[192,192]{1,0:T(8,128)(2,1)S(1)}, bf16[192,192]{1,0:T(8,128)(2,1)S(1)}, u32[]{:S(2)}, u32[]{:S(2)}) collective-permute-start(bf16[192,192]{1,0:T(8,128)(2,1)S(1)} %get-tuple-element.56), channel_id=1, source_target_pairs={{0,16},{16,32},{32,48},{48,0},{64,80},{80,96},{96,112},{112,64},{1... | collective-permute-start | bytes 221192 | tf_op jit(solution)/shard_map/ppermute | solution.py:327
  93.5 19.0 %collective-permute-start.14 = (bf16[192,192]{1,0:T(8,128)(2,1)S(1)}, bf16[192,192]{1,0:T(8,128)(2,1)S(1)}, u32[]{:S(2)}, u32[]{:S(2)}) collective-permute-start(bf16[192,192]{1,0:T(8,128)(2,1)S(1)} %get-tuple-element.57), channel_id=1, source_target_pairs={{0,32},{16,48},{32,0},{48,16},{64,96},{80,112},{96,64},{112,80},{1... | collective-permute-start | bytes 221192 | tf_op jit(solution)/shard_map/ppermute | solution.py:327
  100.0 12.5 %collective-permute-start.15 = (bf16[192,192]{1,0:T(8,128)(2,1)S(1)}, bf16[192,192]{1,0:T(8,128)(2,1)S(1)}, u32[]{:S(2)}, u32[]{:S(2)}) collective-permute-start(bf16[192,192]{1,0:T(8,128)(2,1)S(1)} %get-tuple-element.58), channel_id=1, source_target_pairs={{0,48},{16,0},{32,16},{48,32},{64,112},{80,64},{96,80},{112,96},{1... | collective-permute-start | bytes 221192 | tf_op jit(solution)/shard_map/ppermute | solution.py:327
  102.2 24.4 %collective-permute-start.22 = (bf16[96,1536]{1,0:T(8,128)(2,1)S(1)}, bf16[96,1536]{1,0:T(8,128)(2,1)S(1)}, u32[]{:S(2)}, u32[]{:S(2)}) collective-permute-start(bf16[96,1536]{1,0:T(8,128)(2,1)S(1)} %get-tuple-element.78), channel_id=1, source_target_pairs={{0,4},{1,5},{2,6},{3,7},{4,8},{5,9},{6,10},{7,11},{8,12},{9,13},{1... | collective-permute-start | bytes 884744 | tf_op jit(solution)/shard_map/ppermute | solution.py:335
  105.4 21.3 %collective-permute-start.23 = (bf16[96,1536]{1,0:T(8,128)(2,1)S(1)}, bf16[96,1536]{1,0:T(8,128)(2,1)S(1)}, u32[]{:S(2)}, u32[]{:S(2)}) collective-permute-start(bf16[96,1536]{1,0:T(8,128)(2,1)S(1)} %get-tuple-element.79), channel_id=1, source_target_pairs={{0,8},{1,9},{2,10},{3,11},{4,12},{5,13},{6,14},{7,15},{8,0},{9,1},... | collective-permute-start | bytes 884744 | tf_op jit(solution)/shard_map/ppermute | solution.py:335
  108.7 17.9 %collective-permute-start.24 = (bf16[96,1536]{1,0:T(8,128)(2,1)S(1)}, bf16[96,1536]{1,0:T(8,128)(2,1)S(1)}, u32[]{:S(2)}, u32[]{:S(2)}) collective-permute-start(bf16[96,1536]{1,0:T(8,128)(2,1)S(1)} %get-tuple-element.80), channel_id=1, source_target_pairs={{0,12},{1,13},{2,14},{3,15},{4,0},{5,1},{6,2},{7,3},{8,4},{9,5},{1... | collective-permute-start | bytes 884744 | tf_op jit(solution)/shard_map/ppermute | solution.py:335
  120.6 12.1 %copy-start.2 = (bf16[768,192]{1,0:T(8,128)(2,1)}, bf16[768,192]{1,0:T(8,128)(2,1)S(1)}, u32[]{:S(2)}) copy-start(bf16[768,192]{1,0:T(8,128)(2,1)S(1)} %get-tuple-element.64.dq) | copy-start | bytes 884740
  120.6 22.3 %collective-permute-start.16 = (bf16[384,384]{1,0:T(8,128)(2,1)}, bf16[384,384]{1,0:T(8,128)(2,1)}, u32[]{:S(2)}, u32[]{:S(2)}) collective-permute-start(bf16[384,384]{1,0:T(8,128)(2,1)} %get-tuple-element.66), channel_id=1, source_target_pairs={{0,64},{16,80},{32,96},{48,112},{64,128},{80,144},{96,160},{112,17... | collective-permute-start | bytes 884744 | tf_op jit(solution)/shard_map/ppermute | solution.py:332
  125.3 17.6 %collective-permute-start.17 = (bf16[384,384]{1,0:T(8,128)(2,1)}, bf16[384,384]{1,0:T(8,128)(2,1)}, u32[]{:S(2)}, u32[]{:S(2)}) collective-permute-start(bf16[384,384]{1,0:T(8,128)(2,1)} %get-tuple-element.67), channel_id=1, source_target_pairs={{64,0},{80,16},{96,32},{112,48},{128,64},{144,80},{160,96},{176,11... | collective-permute-start | bytes 884744 | tf_op jit(solution)/shard_map/ppermute | solution.py:332
  126.8 5.9 %collective-permute-start.25 = (bf16[48,1536]{1,0:T(8,128)(2,1)S(1)}, bf16[48,1536]{1,0:T(8,128)(2,1)S(1)}, u32[]{:S(2)}, u32[]{:S(2)}) collective-permute-start(bf16[48,1536]{1,0:T(8,128)(2,1)S(1)} %get-tuple-element.82), channel_id=1, source_target_pairs={{0,2},{1,3},{2,0},{3,1},{4,6},{5,7},{6,4},{7,5},{8,10},{9,11},{10,... | collective-permute-start | bytes 442376 | tf_op jit(solution)/shard_map/ppermute | solution.py:338
  133.5 25.8 %all-to-all-start = ((bf16[8,48,192]{2,1,0:T(8,128)(2,1)}), bf16[8,48,192]{2,1,0:T(8,128)(2,1)}, u32[]{:S(2)}, u32[]{:S(2)}) async-start(bf16[8,48,192]{2,1,0:T(8,128)(2,1)} %copy-done), calls=%async_computation | async-start | bytes 393216 | tf_op jit(solution)/shard_map/all_to_all | solution.py:433
  146.7 23.4 %collective-permute-start.18 = (bf16[192,576]{1,0:T(8,128)(2,1)}, bf16[192,576]{1,0:T(8,128)(2,1)S(1)}, u32[]{:S(2)}, u32[]{:S(2)}) collective-permute-start(bf16[192,576]{1,0:T(8,128)(2,1)} %get-tuple-element.69), channel_id=1, source_target_pairs={{0,16},{16,32},{32,48},{48,0},{64,80},{80,96},{96,112},{112,64},{1... | collective-permute-start | bytes 663560 | tf_op jit(solution)/shard_map/ppermute | solution.py:327
  151.0 19.9 %collective-permute-start.19 = (bf16[192,576]{1,0:T(8,128)(2,1)}, bf16[192,576]{1,0:T(8,128)(2,1)S(1)}, u32[]{:S(2)}, u32[]{:S(2)}) collective-permute-start(bf16[192,576]{1,0:T(8,128)(2,1)} %get-tuple-element.70), channel_id=1, source_target_pairs={{0,32},{16,48},{32,0},{48,16},{64,96},{80,112},{96,64},{112,80},{1... | collective-permute-start | bytes 663560 | tf_op jit(solution)/shard_map/ppermute | solution.py:327
  153.8 24.4 %collective-permute-start.20 = (bf16[192,576]{1,0:T(8,128)(2,1)}, bf16[192,576]{1,0:T(8,128)(2,1)S(1)}, u32[]{:S(2)}, u32[]{:S(2)}) collective-permute-start(bf16[192,576]{1,0:T(8,128)(2,1)} %get-tuple-element.71), channel_id=1, source_target_pairs={{0,48},{16,0},{32,16},{48,32},{64,112},{80,64},{96,80},{112,96},{1... | collective-permute-start | bytes 663560 | tf_op jit(solution)/shard_map/ppermute | solution.py:327
  161.1 22.6 %all-to-all-start.1 = ((bf16[4,2,1152]{2,1,0:T(2,128)(2,1)}), bf16[4,2,1152]{2,1,0:T(2,128)(2,1)S(1)}, u32[]{:S(2)}, u32[]{:S(2)}) async-start(bf16[4,2,1152]{2,1,0:T(2,128)(2,1)} %reshape.10), calls=%async_computation.1 | async-start | bytes 36864 | tf_op jit(solution)/shard_map/all_to_all | solution.py:435
  (20 other events, 71.0 us)

commit v2 on v1

v2 whole, which is shorter than its diff:
```python
import jax
import jax.numpy as jnp
from jax import lax
from jax.experimental import pallas as pl
from jax.experimental.pallas import tpu as pltpu
from jax.sharding import PartitionSpec as P

HEAD_DIM = 96
ROWS = 192
GROUP = 4
PAIR = 2 * HEAD_DIM
INNER = GROUP * PAIR
OWN = GROUP * ROWS
REACH = 2 * ROWS
SPAN = OWN + 2 * REACH
TILE = 256
WINDOW = TILE + 2 * REACH
STRIP = 48
WIDTH = 1536
SCALE = HEAD_DIM ** (-0.5)
LOG2E = 1.4426950408889634
NEG_FILL = -1e30
BF16 = jnp.bfloat16
F32 = jnp.float32


def struct(shape, dtype=BF16):
    return jax.ShapeDtypeStruct(shape, dtype)


def call(body, out_shape, args, flops=0, scratch=(), smem=1, near=False):
    scalars = pl.BlockSpec(memory_space=pltpu.SMEM)

    def whole(a):
        if near:
            return pl.BlockSpec(memory_space=pltpu.VMEM)
        return pl.BlockSpec(a.shape, lambda step: (0,) * len(a.shape))

    moved = sum(a.size * a.dtype.itemsize for a in args)
    moved += sum(o.size * o.dtype.itemsize for o in jax.tree.leaves(out_shape))
    return pl.pallas_call(
        body,
        out_shape=out_shape,
        grid=() if near else (1,),
        in_specs=[scalars] * smem + [whole(a) for a in args[smem:]],
        out_specs=jax.tree.map(whole, out_shape),
        scratch_shapes=list(scratch),
        cost_estimate=pl.CostEstimate(flops=flops, bytes_accessed=moved, transcendentals=0),
        compiler_params=pltpu.CompilerParams(
            vmem_limit_bytes=(16 if near else 60) * 1024 * 1024
        ),
    )(*args)


def wrap(index):
    return lax.rem(index + 2 * GROUP, GROUP)


def rows_at(start, size):
    return pl.ds(pl.multiple_of(start, 16), size)


def dot(a, b):
    return jnp.dot(a, b, preferred_element_type=F32)


def dot_nt(a, b):
    return lax.dot_general(a, b, (((1,), (1,)), ((), ())), preferred_element_type=F32)


def pack_heads(q, k, v, out):
    for pair in range(GROUP):
        columns = slice(pair * PAIR, (pair + 1) * PAIR)
        rows = slice(pair * ROWS, (pair + 1) * ROWS)
        out[rows, 0:PAIR] = k[0, :, columns]
        out[rows, PAIR : 2 * PAIR] = v[0, :, columns]
        out[rows, 2 * PAIR : 3 * PAIR] = q[0, :, columns]


def pack_edges(parts, low, high):
    low[...] = parts[0:REACH, 0 : 2 * PAIR]
    high[...] = parts[OWN - REACH : OWN, 0 : 2 * PAIR]


def tile_mask(lengths, first_query, frames):
    query = first_query + lax.broadcasted_iota(jnp.int32, (TILE, 1), 0)
    low = jnp.maximum(query - REACH, 0)
    high = jnp.minimum(query + REACH, frames - 1)
    end = 0
    for recording in range(3):
        end = end + lengths[0, recording]
        low = jnp.maximum(low, jnp.where(query >= end, end, 0))
        high = jnp.minimum(high, jnp.where(query < end, end - 1, frames - 1))
    key = first_query - REACH + lax.broadcasted_iota(jnp.int32, (1, WINDOW), 1)
    return (key >= low) & (key <= high)


def head_columns(head):
    lane = lax.broadcasted_iota(jnp.int32, (1, PAIR), 1)
    return (lane >= head * HEAD_DIM) & (lane < (head + 1) * HEAD_DIM)


def forward(frames, pos, lengths, parts, before, after, q_all, k_all, v_all, context, log_total):
    z = pos[1]
    k_all[0:REACH, :] = before[:, 0:PAIR]
    v_all[0:REACH, :] = before[:, PAIR : 2 * PAIR]
    k_all[REACH + OWN : SPAN, :] = after[:, 0:PAIR]
    v_all[REACH + OWN : SPAN, :] = after[:, PAIR : 2 * PAIR]
    k_all[REACH : REACH + OWN, :] = parts[:, 0:PAIR]
    v_all[REACH : REACH + OWN, :] = parts[:, PAIR : 2 * PAIR]
    q_all[...] = parts[:, 2 * PAIR : 3 * PAIR]

    def step(tile, _):
        first = pl.multiple_of(tile * TILE, TILE)
        mask = tile_mask(lengths, z * OWN + first, frames)
        query = q_all[pl.ds(first, TILE), :]
        keys = k_all[pl.ds(first, WINDOW), :]
        values = v_all[pl.ds(first, WINDOW), :]
        lane = lax.broadcasted_iota(jnp.int32, (TILE, 128), 1)
        total = jnp.zeros((TILE, PAIR), F32)
        logs = jnp.zeros((TILE, 128), F32)
        for head in range(2):
            inside = head_columns(head)
            scores = dot_nt(jnp.where(inside, query, 0), keys)
            scores = jnp.where(mask, scores, NEG_FILL)
            largest = jnp.max(scores, axis=1, keepdims=True)
            expo = jnp.exp2((scores - largest) * (SCALE * LOG2E))
            sums = jnp.sum(expo, axis=1, keepdims=True)
            product = dot(expo.astype(BF16), values) / sums
            total = jnp.where(inside, product, total)
            logs = jnp.where(lane == head, largest + jnp.log(sums) * (1.0 / SCALE), logs)
        context[pl.ds(first, TILE), :] = total.astype(BF16)
        log_total[pl.ds(first, TILE), :] = logs
        return 0

    lax.fori_loop(0, OWN // TILE, step, 0)


def backward(frames, pos, lengths, q_all, k_all, v_all, context, log_total, *refs):
    parts = refs[:GROUP]
    dq, own, low, high, dk, dv, dcontext = refs[GROUP:]
    y = pos[0]
    for hop in range(GROUP):
        dcontext[rows_at(wrap(y - hop) * ROWS, ROWS), :] = parts[hop][...]
    z = pos[1]
    dk[...] = jnp.zeros_like(dk)
    dv[...] = jnp.zeros_like(dv)

    def step(tile, _):
        first = pl.multiple_of(tile * TILE, TILE)
        mask = tile_mask(lengths, z * OWN + first, frames)
        query = q_all[pl.ds(first, TILE), :]
        keys = k_all[pl.ds(first, WINDOW), :]
        values = v_all[pl.ds(first, WINDOW), :]
        grads = dcontext[pl.ds(first, TILE), :]
        product = grads.astype(F32) * context[pl.ds(first, TILE), :].astype(F32)
        logs = log_total[pl.ds(first, TILE), :]
        query_t = query.T
        grads_t = grads.T
        total = jnp.zeros((TILE, PAIR), F32)
        for head in range(2):
            inside = head_columns(head)
            own_rows = slice(head * HEAD_DIM, (head + 1) * HEAD_DIM)
            delta = jnp.sum(jnp.where(inside, product, 0.0), axis=1, keepdims=True)
            scores = dot_nt(jnp.where(inside, query, 0), keys)
            scores = jnp.where(mask, scores, NEG_FILL)
            probability = jnp.exp2((scores - logs[:, head : head + 1]) * (SCALE * LOG2E))
            gap = dot_nt(jnp.where(inside, grads, 0), values) - delta
            score_grad = (probability * gap).astype(BF16)
            total = jnp.where(inside, dot(score_grad, keys), total)
            dk[own_rows, pl.ds(first, WINDOW)] += dot(query_t[own_rows, :], score_grad)
            dv[own_rows, pl.ds(first, WINDOW)] += dot(
                grads_t[own_rows, :], probability.astype(BF16)
            )
        dq[pl.ds(first, TILE), :] = (total * SCALE).astype(BF16)
        return 0

    lax.fori_loop(0, OWN // TILE, step, 0)
    low[:, 0:PAIR] = (dk[:, 0:REACH].T * SCALE).astype(BF16)
    low[:, PAIR : 2 * PAIR] = dv[:, 0:REACH].T.astype(BF16)
    high[:, 0:PAIR] = (dk[:, REACH + OWN : SPAN].T * SCALE).astype(BF16)
    high[:, PAIR : 2 * PAIR] = dv[:, REACH + OWN : SPAN].T.astype(BF16)
    own[:, 0:PAIR] = dk[:, REACH : REACH + OWN].T * SCALE
    own[:, PAIR : 2 * PAIR] = dv[:, REACH : REACH + OWN].T


def pack_grads(pos, dq, own, from_before, from_after, *refs):
    outs, total = refs[:GROUP], refs[GROUP]
    y = pos[0]
    first, last = slice(0, REACH), slice(REACH, OWN)
    total[first, :] = own[first, :] + from_before[...].astype(F32)
    total[last, :] = own[last, :] + from_after[...].astype(F32)
    for hop in range(GROUP):
        rows = rows_at(wrap(y + hop) * ROWS, ROWS)
        outs[hop][:, 0 : 2 * PAIR] = total[rows, :].astype(BF16)
        outs[hop][:, 2 * PAIR : 3 * PAIR] = dq[rows, :]


def unpack_grads(pos, *refs):
    parts, (dq, dk, dv) = refs[:GROUP], refs[GROUP:]
    y = pos[0]
    for hop in range(GROUP):
        shard = wrap(y - hop)
        for pair in range(GROUP):

            @pl.when(shard == pair)
            def _(hop=hop, pair=pair):
                columns = slice(pair * PAIR, (pair + 1) * PAIR)
                dk[0, :, columns] = parts[hop][:, 0:PAIR]
                dv[0, :, columns] = parts[hop][:, PAIR : 2 * PAIR]
                dq[0, :, columns] = parts[hop][:, 2 * PAIR : 3 * PAIR]


def join(*refs):
    parts, out = refs[:-1], refs[-1]
    size = parts[0].shape[0]
    for j, part in enumerate(parts):
        out[j * size : (j + 1) * size, :] = part[...]


def context_grad(pos, cot, mine, other, weight, *outs):
    y, x, y_low, core = pos[0], pos[2], pos[3], pos[4]
    for j in range(4):
        for t in range(2):
            for flip, source in ((0, mine), (1, other)):
                strip = wrap(x - j) * 4 + (y_low + t) % 2 * 2 + (core + flip) % 2
                start = j * 2 * STRIP + t * STRIP
                weight[rows_at(strip * STRIP, STRIP), :] = source[start : start + STRIP, :]
    for hop in range(GROUP):
        rows = rows_at(wrap(y + hop) * PAIR, PAIR)
        outs[hop][...] = dot_nt(cot[0], weight[rows, :]).astype(BF16)


def weight_term(pos, cot, context, keep, send):
    core = pos[4]
    for pair in range(GROUP):
        part = context[pair * ROWS : (pair + 1) * ROWS, :]
        term = dot(part.T, cot[0]).astype(BF16)
        for i in range(4):
            start = (pair * 2 + i // 2) * STRIP
            rows = slice(start, start + STRIP)
            value = term[i * STRIP : (i + 1) * STRIP, :]

            @pl.when(core == i % 2)
            def _(rows=rows, value=value):
                keep[rows, :] = value

            @pl.when(core != i % 2)
            def _(rows=rows, value=value):
                send[rows, :] = value


def project(weight, context, attended):
    for block in range(3):
        columns = slice(block * 512, (block + 1) * 512)
        total = jnp.zeros((ROWS, 512), F32)
        for pair in range(GROUP):
            rows = slice(pair * ROWS, (pair + 1) * ROWS)
            total = total + dot(context[rows, :], weight[rows, columns])
        attended[0, :, columns] = total.astype(BF16)


def add_cores(keep, received, out):
    out[...] = (keep[...].astype(F32) + received[...].astype(F32)).astype(BF16)


def added(parts, size):
    total = parts[0:size, :].astype(F32)
    for j in range(1, parts.shape[0] // size):
        total = total + parts[j * size : (j + 1) * size, :].astype(F32)
    return total


def add_x(parts, out):
    total = added(parts, 2 * STRIP).astype(BF16)
    for shard in range(GROUP):
        for strip in range(2):
            start = (shard * 2 + strip) * STRIP
            value = total[strip * STRIP : (strip + 1) * STRIP, :]
            for z in range(out.shape[1] // STRIP):
                source = (z * GROUP + shard) * STRIP
                out[start : start + STRIP, z * STRIP : (z + 1) * STRIP] = value[
                    :, source : source + STRIP
                ]


def add_y(parts, out):
    total = added(parts, STRIP).astype(BF16)
    out[...] = jnp.zeros_like(out)
    for z in range(total.shape[1] // STRIP):
        out[z * STRIP : (z + 1) * STRIP, 0:STRIP] = total[:, z * STRIP : (z + 1) * STRIP]


def add_z(parts, out):
    out[...] = added(parts, STRIP)[:, 0:STRIP]


def on_device(queries, keys, values, rec_lengths, out_weight, cotangent):
    n_seq = lax.axis_size("seq")
    n_z = n_seq // GROUP
    frames = n_seq * ROWS
    seq_index = lax.axis_index("seq")
    strip_index = lax.axis_index("fsdp")
    pos = jnp.stack(
        [
            seq_index % GROUP,
            seq_index // GROUP,
            strip_index // 4,
            strip_index // 2 % 2,
            strip_index % 2,
        ]
    ).astype(jnp.int32)
    y_groups = [[z * GROUP + y for y in range(GROUP)] for z in range(n_z)]
    x_groups = [[x * 4 + rest for x in range(4)] for rest in range(4)]
    z_groups = [[z * GROUP + y for z in range(n_z)] for y in range(GROUP)]
    whole_y_groups = [
        [(z * GROUP + y) * 16 + x * 4 + y_low * 2 + core for y in range(GROUP) for y_low in range(2)]
        for z in range(n_z)
        for x in range(4)
        for core in range(2)
    ]

    def exchange(block, axis="seq", groups=y_groups):
        return lax.all_to_all(block, axis, 0, 0, axis_index_groups=groups, tiled=True)

    def along_z(block, hop):
        moved = hop * GROUP
        route = [(i, i + moved) for i in range(n_seq) if 0 <= i + moved < n_seq]
        return lax.ppermute(block, "seq", route)

    def along_y(block, hop):
        route = [(i, i // GROUP * GROUP + (i + hop) % GROUP) for i in range(n_seq)]
        return lax.ppermute(block, "seq", route)

    def along_x(block, hop):
        return lax.ppermute(block, "fsdp", [(i, (i + 4 * hop) % 16) for i in range(16)])

    def swap_y_low(block):
        return lax.ppermute(block, "fsdp", [(i, i ^ 2) for i in range(16)])

    def swap_core(block):
        return lax.ppermute(block, "fsdp", [(i, i ^ 1) for i in range(16)])

    def spread(chunks):
        return [chunks[0]] + [along_y(chunks[hop], hop) for hop in range(1, GROUP)]

    together = lax.optimization_barrier
    half = struct((INNER // 2, WIDTH))
    edge = struct((REACH, 2 * PAIR))
    square = struct((OWN, PAIR))
    span = struct((SPAN, PAIR))
    chunk = struct((ROWS, 3 * PAIR))
    full = struct((1, ROWS, INNER))
    pair_flops = 2 * 2 * OWN * WINDOW * PAIR
    project_flops = 2 * ROWS * INNER * WIDTH

    packed = call(pack_heads, struct((OWN, 3 * PAIR)), (queries, keys, values), smem=0)
    other_strip = swap_y_low(out_weight)
    packed, other_strip = together((packed, other_strip))
    parts = exchange(packed)
    strips = call(
        join, struct((2 * STRIP, WIDTH)), (out_weight, other_strip), smem=0, near=True
    )
    weights = [along_x(strips, hop) for hop in (1, 2, 3)]
    parts, weights = together((parts, weights))

    low, high = call(pack_edges, (edge, edge), (parts,), smem=0, near=True)
    after, before = along_z(low, -1), along_z(high, 1)
    mine = call(join, half, (strips, *weights), smem=0, near=True)
    mine, before, after = together((mine, before, after))
    other = swap_core(mine)
    q_all, k_all, v_all, context, log_total = call(
        lambda *refs: forward(frames, *refs),
        (square, span, span, square, struct((OWN, 128), F32)),
        (pos, rec_lengths, parts, before, after),
        flops=2 * pair_flops,
        smem=2,
    )
    context_rows = exchange(context)
    mine, context = together((mine, context))
    weight, *grads = call(
        context_grad,
        (struct((INNER, WIDTH)),) + (struct((ROWS, PAIR)),) * GROUP,
        (pos, cotangent, mine, other),
        flops=project_flops,
    )
    grads = spread(grads)
    context_rows, grads = together((context_rows, grads))

    keep, send = call(
        weight_term, (half, half), (pos, cotangent, context_rows), flops=project_flops
    )
    received = swap_core(send)
    keep, grads, context_rows = together((keep, grads, context_rows))
    dq, own, low, high = call(
        lambda *refs: backward(frames, *refs),
        (square, struct((OWN, 2 * PAIR), F32), edge, edge),
        (pos, rec_lengths, q_all, k_all, v_all, context, log_total, *grads),
        flops=5 * pair_flops,
        scratch=[
            pltpu.VMEM((PAIR, SPAN), F32),
            pltpu.VMEM((PAIR, SPAN), F32),
            pltpu.VMEM((OWN, PAIR), BF16),
        ],
        smem=2,
    )
    received, low, high = together((received, low, high))
    from_after, from_before = along_z(low, -1), along_z(high, 1)
    sums = call(add_cores, half, (keep, received), smem=0)
    sums = exchange(sums, "fsdp", x_groups)
    chunks = call(
        pack_grads,
        (chunk,) * GROUP,
        (pos, dq, own, from_before, from_after),
        scratch=[pltpu.VMEM((OWN, 2 * PAIR), F32)],
    )
    sums, chunks = together((sums, chunks))
    sums = call(add_x, struct((2 * GROUP * STRIP, n_z * STRIP)), (sums,), smem=0, near=True)
    grads = spread(chunks)
    sums = exchange(sums, ("seq", "fsdp"), whole_y_groups)
    sums = call(add_y, struct((n_z * STRIP, 128)), (sums,), smem=0, near=True)
    sums, context_rows = together((sums, context_rows))
    sums = exchange(sums, "seq", z_groups)
    attended = call(
        project, struct((1, ROWS, WIDTH)), (weight, context_rows), flops=project_flops, smem=0
    )
    attended, grads = together((attended, grads))
    grad_queries, grad_keys, grad_values = call(unpack_grads, (full, full, full), (pos, *grads))
    sums, grad_queries = together((sums, grad_queries))
    grad_weight = call(add_z, struct((STRIP, STRIP), F32), (sums,), smem=0, near=True)
    return attended, grad_queries, grad_keys, grad_values, grad_weight


def solution(mesh):
    rows = P("fsdp", "seq", None)
    return jax.shard_map(
        on_device,
        mesh=mesh,
        in_specs=(rows, rows, rows, P("fsdp", None), P("fsdp", None), rows),
        out_specs=(rows, rows, rows, rows, P("fsdp", "seq")),
        check_vma=False,
    )
```

time: 186 us -> 183 us (0.984)
  starting transfers between devices: 111 us -> 87.6 us
  waiting for transfers between devices: 32.1 us -> 48.7 us
  Pallas kernels: 26.9 us -> 40.8 us
  local copies, waits for them, and re-layouts: 12.8 us -> 4.15 us
    ppermute x12 -> x6, starting transfers between devices: 53.3 us -> 29.3 us  [along_y(): return lax.ppermute(block, 'seq', route)]
    all_to_all x2 -> x5, starting transfers between devices: 12.7 us -> 27.9 us  [exchange(): lax.all_to_all(block, axis, 0, 0, axis_index_groups=groups, tiled=True)]
    pallas_call x14 -> x15, Pallas kernels: 26.9 us -> 40.8 us  [call(): pl.pallas_call(body, out_shape=out_shape, grid=() if near else (1,), in_s...]
    ppermute x6 -> x3, waiting for transfers between devices: 0.02 us -> 13.1 us  [along_x(): lax.ppermute(block, 'fsdp', [(i, (i + 4 * hop) % 16) for i in range(16)])]
    ppermute x6 -> x3, starting transfers between devices: 21.7 us -> 9.33 us  [along_x(): lax.ppermute(block, 'fsdp', [(i, (i + 4 * hop) % 16) for i in range(16)])]
    ppermute x4, waiting for transfers between devices: 9.22 us -> 19.9 us  [along_z(): return lax.ppermute(block, 'seq', route)]
    unnamed x53 -> x42, local copies, waits for them, and re-layouts: 12.7 us -> 3.48 us
    ppermute x2 -> x1, waiting for transfers between devices: 5.74 us -> 0.39 us  [swap_y_low(): return lax.ppermute(block, 'fsdp', [(i, i ^ 2) for i in range(16)])]
  transfers between devices with their start and end apart: 28 -> 21, of which waited for: 7 -> 12; matrix products, arithmetic and copies ran while one was open for 1% -> 0% of each run, Pallas kernels for 14% -> 17%
where the time goes in v2:
time: 183 us; the launch traced here: 182 us
  starting transfers between devices  87.6 us (48%)
  waiting for transfers between devices  48.7 us (27%)
  Pallas kernels  40.8 us (22%)
  local copies, waits for them, and re-layouts  4.15 us (2%)
    pallas_call x15, Pallas kernels, call(): pl.pallas_call(body, out_shape=out_shape, grid=() if near else (1,), in_s...  40.8 us
    ppermute x6, starting transfers between devices, along_y(): return lax.ppermute(block, 'seq', route)  29.3 us
    all_to_all x5, starting transfers between devices, exchange(): lax.all_to_all(block, axis, 0, 0, axis_index_groups=groups, tiled=True)  27.9 us
    ppermute x4, waiting for transfers between devices, along_z(): return lax.ppermute(block, 'seq', route)  19.9 us
    ppermute x6, waiting for transfers between devices, along_y(): return lax.ppermute(block, 'seq', route)  13.3 us
    ppermute x3, waiting for transfers between devices, along_x(): lax.ppermute(block, 'fsdp', [(i, (i + 4 * hop) % 16) for i in range(16)])  13.1 us
    ppermute x4, starting transfers between devices, along_z(): return lax.ppermute(block, 'seq', route)  10.8 us
    ppermute x3, starting transfers between devices, along_x(): lax.ppermute(block, 'fsdp', [(i, (i + 4 * hop) % 16) for i in range(16)])  9.33 us
  transfers between devices with their start and end apart: 21, of which 12 were waited for; matrix products, arithmetic and copies ran while one was open for 0% of the time, Pallas kernels for 17%

profile of v2, /device:TPU:1, one launch (start us, length us, event | category | flops | bytes accessed | tf_op | source)
XLA Modules:
  0.0 182.3 jit_solution(9638122347230696391)
XLA Ops:
  0.6 4.0 %collective-permute-start = (bf16[48,1536]{1,0:T(8,128)(2,1)}, bf16[48,1536]{1,0:T(8,128)(2,1)S(1)}, u32[]{:S(2)}, u32[]{:S(2)}) collective-permute-start(bf16[48,1536]{1,0:T(8,128)(2,1)} %refs_0_.1), channel_id=1, source_target_pairs={{0,2},{1,3},{2,0},{3,1},{4,6},{5,7},{6,4},{7,5},{8,10},{9,11},{10,... | collective-permute-start | bytes 442376 | tf_op jit(solution)/shard_map/ppermute | solution.py:339
  7.4 7.7 %all-to-all-start = ((bf16[4,192,576]{2,1,0:T(8,128)(2,1)}), bf16[4,192,576]{2,1,0:T(8,128)(2,1)S(1)}, u32[]{:S(2)}, u32[]{:S(2)}) async-start(bf16[4,192,576]{2,1,0:T(8,128)(2,1)} %bitcast.21), calls=%async_computation | async-start | bytes 1966080 | tf_op jit(solution)/shard_map/all_to_all | solution.py:324
  15.1 4.4 %collective-permute-start.3 = (bf16[96,1536]{1,0:T(8,128)(2,1)S(1)}, bf16[96,1536]{1,0:T(8,128)(2,1)S(1)}, u32[]{:S(2)}, u32[]{:S(2)}) collective-permute-start(bf16[96,1536]{1,0:T(8,128)(2,1)S(1)} %shard_map.102.refs_0_), channel_id=1, source_target_pairs={{0,12},{1,13},{2,14},{3,15},{4,0},{5,1},{6,2},{7,3},{8,4},{9,5},{1... | collective-permute-start | bytes 884744 | tf_op jit(solution)/shard_map/ppermute | solution.py:336
  24.8 4.5 %collective-permute-done.2.refs_2_ = bf16[96,1536]{1,0:T(8,128)(2,1)S(1)} collective-permute-done((bf16[96,1536]{1,0:T(8,128)(2,1)S(1)}, bf16[96,1536]{1,0:T(8,128)(2,1)S(1)}, u32[]{:S(2)}, u32[]{:S(2)}) %collective-permute-start.2) | collective-permute-done | bytes 294944 | tf_op jit(solution)/shard_map/ppermute | solution.py:336
  29.3 8.2 %collective-permute-done.1.refs_1_ = bf16[96,1536]{1,0:T(8,128)(2,1)S(1)} collective-permute-done((bf16[96,1536]{1,0:T(8,128)(2,1)S(1)}, bf16[96,1536]{1,0:T(8,128)(2,1)S(1)}, u32[]{:S(2)}, u32[]{:S(2)}) %collective-permute-start.1) | collective-permute-done | bytes 294944 | tf_op jit(solution)/shard_map/ppermute | solution.py:336
  39.6 4.2 %collective-permute-start.4 = (bf16[384,384]{1,0:T(8,128)(2,1)S(1)}, bf16[384,384]{1,0:T(8,128)(2,1)S(1)}, u32[]{:S(2)}, u32[]{:S(2)}) collective-permute-start(bf16[384,384]{1,0:T(8,128)(2,1)S(1)} %get-tuple-element.75), channel_id=1, source_target_pairs={{0,64},{16,80},{32,96},{48,112},{64,128},{80,144},{96,160},{112,17... | collective-permute-start | bytes 884744 | tf_op jit(solution)/shard_map/ppermute | solution.py:329
  45.3 4.3 %collective-permute-done.4.refs_3_ = bf16[384,384]{1,0:T(8,128)(2,1)S(1)} collective-permute-done((bf16[384,384]{1,0:T(8,128)(2,1)S(1)}, bf16[384,384]{1,0:T(8,128)(2,1)S(1)}, u32[]{:S(2)}, u32[]{:S(2)}) %collective-permute-start.4) | collective-permute-done | bytes 294944 | tf_op jit(solution)/shard_map/ppermute | solution.py:329
  49.6 4.8 %collective-permute-done.5.refs_4_ = bf16[384,384]{1,0:T(8,128)(2,1)S(1)} collective-permute-done((bf16[384,384]{1,0:T(8,128)(2,1)S(1)}, bf16[384,384]{1,0:T(8,128)(2,1)S(1)}, u32[]{:S(2)}, u32[]{:S(2)}) %collective-permute-start.5) | collective-permute-done | bytes 294944 | tf_op jit(solution)/shard_map/ppermute | solution.py:329
  54.3 3.4 %collective-permute-start.6 = (bf16[384,1536]{1,0:T(8,128)(2,1)S(1)}, bf16[384,1536]{1,0:T(8,128)(2,1)S(1)}, u32[]{:S(2)}, u32[]{:S(2)}) collective-permute-start(bf16[384,1536]{1,0:T(8,128)(2,1)S(1)} %shard_map.103.mine), channel_id=1, source_target_pairs={{0,1},{1,0},{2,3},{3,2},{4,5},{5,4},{6,7},{7,6},{8,9},{9,8},{10,11... | collective-permute-start | bytes 3538952 | tf_op jit(solution)/shard_map/ppermute | solution.py:342
  58.4 6.8 %shard_map.105 = (bf16[768,192]{1,0:T(8,128)(2,1)}, bf16[1536,192]{1,0:T(8,128)(2,1)}, bf16[1536,192]{1,0:T(8,128)(2,1)}, bf16[768,192]{1,0:T(8,128)(2,1)}, f32[768,128]{1,0:T(8,128)}) custom-call(s32[5]{0:T(128)} %stack.23.refs_0_.pos, s32[1,4]{1,0:T(1,128)} %refs_1_.3, bf16[768,576]{1,0:T(8,128)(2,1)} %bitcast.17, bf16[384,384]{1,0:T(8,128)(2,1)} %copy-done.11, ...), custom_call_target="tpu_custom_call" | custom-call | flops 1207959552 | bytes 3637284 | tf_op jit(solution)/shard_map/pallas_call | solution.py:41
  65.2 4.3 %all-to-all-start.1 = ((bf16[4,192,192]{2,1,0:T(8,128)(2,1)}), bf16[4,192,192]{2,1,0:T(8,128)(2,1)S(1)}, u32[]{:S(2)}, u32[]{:S(2)}) async-start(bf16[4,192,192]{2,1,0:T(8,128)(2,1)} %bitcast.24), calls=%async_computation.1 | async-start | bytes 786432 | tf_op jit(solution)/shard_map/all_to_all | solution.py:324
  70.5 3.5 %shard_map.106 = (bf16[768,1536]{1,0:T(8,128)(2,1)}, bf16[192,192]{1,0:T(8,128)(2,1)}, bf16[192,192]{1,0:T(8,128)(2,1)}, bf16[192,192]{1,0:T(8,128)(2,1)}, bf16[192,192]{1,0:T(8,128)(2,1)}) custom-call(s32[5]{0:T(128)} %stack.23.refs_0_.pos, bf16[1,192,1536]{2,1,0:T(8,128)(2,1)} %cot.3, bf16[384,1536]{1,0:T(8,128)(2,1)} %copy-done, bf16[384,1536]{1,0:T(8,128)(2,1)} %copy-done.4), custom_call_target="tpu_custom_call" | custom-call | flops 452984832 | bytes 5603348 | tf_op jit(solution)/shard_map/pallas_call | solution.py:41
  74.0 4.3 %collective-permute-start.7 = (bf16[192,192]{1,0:T(8,128)(2,1)}, bf16[192,192]{1,0:T(8,128)(2,1)S(1)}, u32[]{:S(2)}, u32[]{:S(2)}) collective-permute-start(bf16[192,192]{1,0:T(8,128)(2,1)} %get-tuple-element.84), channel_id=1, source_target_pairs={{0,16},{16,32},{32,48},{48,0},{64,80},{80,96},{96,112},{112,64},{1... | collective-permute-start | bytes 221192 | tf_op jit(solution)/shard_map/ppermute | solution.py:333
  78.2 5.2 %collective-permute-start.8 = (bf16[192,192]{1,0:T(8,128)(2,1)}, bf16[192,192]{1,0:T(8,128)(2,1)S(1)}, u32[]{:S(2)}, u32[]{:S(2)}) collective-permute-start(bf16[192,192]{1,0:T(8,128)(2,1)} %get-tuple-element.85), channel_id=1, source_target_pairs={{0,32},{16,48},{32,0},{48,16},{64,96},{80,112},{96,64},{112,80},{1... | collective-permute-start | bytes 221192 | tf_op jit(solution)/shard_map/ppermute | solution.py:333
  83.5 5.2 %collective-permute-start.9 = (bf16[192,192]{1,0:T(8,128)(2,1)}, bf16[192,192]{1,0:T(8,128)(2,1)S(1)}, u32[]{:S(2)}, u32[]{:S(2)}) collective-permute-start(bf16[192,192]{1,0:T(8,128)(2,1)} %get-tuple-element.86), channel_id=1, source_target_pairs={{0,48},{16,0},{32,16},{48,32},{64,112},{80,64},{96,80},{112,96},{1... | collective-permute-start | bytes 221192 | tf_op jit(solution)/shard_map/ppermute | solution.py:333
  88.7 4.4 %collective-permute-done.9.refs_10_ = bf16[192,192]{1,0:T(8,128)(2,1)S(1)} collective-permute-done((bf16[192,192]{1,0:T(8,128)(2,1)}, bf16[192,192]{1,0:T(8,128)(2,1)S(1)}, u32[]{:S(2)}, u32[]{:S(2)}) %collective-permute-start.9) | collective-permute-done | bytes 73760 | tf_op jit(solution)/shard_map/ppermute | solution.py:333
  93.1 4.3 %shard_map.107 = (bf16[384,1536]{1,0:T(8,128)(2,1)}, bf16[384,1536]{1,0:T(8,128)(2,1)}) custom-call(s32[5]{0:T(128)} %stack.23.refs_0_.pos, bf16[1,192,1536]{2,1,0:T(8,128)(2,1)} %cot.3, bf16[768,192]{1,0:T(8,128)(2,1)} %bitcast.22), custom_call_target="tpu_custom_call" | custom-call | flops 452984832 | bytes 3244052 | tf_op jit(solution)/shard_map/pallas_call | solution.py:41
  97.4 2.8 %collective-permute-start.10 = (bf16[384,1536]{1,0:T(8,128)(2,1)}, bf16[384,1536]{1,0:T(8,128)(2,1)S(1)}, u32[]{:S(2)}, u32[]{:S(2)}) collective-permute-start(bf16[384,1536]{1,0:T(8,128)(2,1)} %get-tuple-element.94), channel_id=1, source_target_pairs={{0,1},{1,0},{2,3},{3,2},{4,5},{5,4},{6,7},{7,6},{8,9},{9,8},{10,11... | collective-permute-start | bytes 3538952 | tf_op jit(solution)/shard_map/ppermute | solution.py:342
  100.3 9.7 %shard_map.108 = (bf16[768,192]{1,0:T(8,128)(2,1)}, f32[768,384]{1,0:T(8,128)}, bf16[384,384]{1,0:T(8,128)(2,1)}, bf16[384,384]{1,0:T(8,128)(2,1)}) custom-call(s32[5]{0:T(128)} %stack.23.refs_0_.pos, s32[1,4]{1,0:T(1,128)} %refs_1_.3, bf16[768,192]{1,0:T(8,128)(2,1)} %get-tuple-element.95.refs_2_, bf16[1536,192]{1,0:T(8,128)(2,1)} %get-tuple-element.96.refs_3_, ...), custom_call_target="tpu_custom_call" | custom-call | flops 3019898880 | bytes 4522020 | tf_op jit(solution)/shard_map/pallas_call | solution.py:41
  110.9 2.9 %shard_map.109 = bf16[384,1536]{1,0:T(8,128)(2,1)} custom-call(bf16[384,1536]{1,0:T(8,128)(2,1)} %get-tuple-element.93.keep, bf16[384,1536]{1,0:T(8,128)(2,1)} %copy-done.5), custom_call_target="tpu_custom_call" | custom-call | bytes 3538944 | tf_op jit(solution)/shard_map/pallas_call | solution.py:41
  113.9 3.7 %all-to-all-start.2 = ((bf16[4,96,1536]{2,1,0:T(8,128)(2,1)}), bf16[4,96,1536]{2,1,0:T(8,128)(2,1)S(1)}, u32[]{:S(2)}, u32[]{:S(2)}) async-start(bf16[4,96,1536]{2,1,0:T(8,128)(2,1)} %bitcast.20), calls=%async_computation.2 | async-start | bytes 2359296 | tf_op jit(solution)/shard_map/all_to_all | solution.py:324
  117.5 4.0 %collective-permute-start.11 = (bf16[384,384]{1,0:T(8,128)(2,1)S(1)}, bf16[384,384]{1,0:T(8,128)(2,1)S(1)}, u32[]{:S(2)}, u32[]{:S(2)}) collective-permute-start(bf16[384,384]{1,0:T(8,128)(2,1)S(1)} %copy-done.14), channel_id=1, source_target_pairs={{0,64},{16,80},{32,96},{48,112},{64,128},{80,144},{96,160},{112,17... | collective-permute-start | bytes 884744 | tf_op jit(solution)/shard_map/ppermute | solution.py:329
  122.9 4.9 %collective-permute-done.11.from_before = bf16[384,384]{1,0:T(8,128)(2,1)S(1)} collective-permute-done((bf16[384,384]{1,0:T(8,128)(2,1)S(1)}, bf16[384,384]{1,0:T(8,128)(2,1)S(1)}, u32[]{:S(2)}, u32[]{:S(2)}) %collective-permute-start.11) | collective-permute-done | bytes 294944 | tf_op jit(solution)/shard_map/ppermute | solution.py:329
  127.8 6.0 %collective-permute-done.12.from_after = bf16[384,384]{1,0:T(8,128)(2,1)S(1)} collective-permute-done((bf16[384,384]{1,0:T(8,128)(2,1)S(1)}, bf16[384,384]{1,0:T(8,128)(2,1)S(1)}, u32[]{:S(2)}, u32[]{:S(2)}) %collective-permute-start.12) | collective-permute-done | bytes 294944 | tf_op jit(solution)/shard_map/ppermute | solution.py:329
  138.3 6.5 %all-to-all-start.3 = ((bf16[8,48,384]{2,1,0:T(8,128)(2,1)}), bf16[8,48,384]{2,1,0:T(8,128)(2,1)S(1)}, u32[]{:S(2)}, u32[]{:S(2)}) async-start(bf16[8,48,384]{2,1,0:T(8,128)(2,1)} %bitcast.11), calls=%async_computation.3 | async-start | bytes 589824 | tf_op jit(solution)/shard_map/all_to_all | solution.py:324
  144.8 4.3 %collective-permute-start.13 = (bf16[192,576]{1,0:T(8,128)(2,1)S(1)}, bf16[192,576]{1,0:T(8,128)(2,1)S(1)}, u32[]{:S(2)}, u32[]{:S(2)}) collective-permute-start(bf16[192,576]{1,0:T(8,128)(2,1)S(1)} %copy-done.17), channel_id=1, source_target_pairs={{0,16},{16,32},{32,48},{48,0},{64,80},{80,96},{96,112},{112,64},{1... | collective-permute-start | bytes 663560 | tf_op jit(solution)/shard_map/ppermute | solution.py:333
  149.1 5.2 %collective-permute-start.14 = (bf16[192,576]{1,0:T(8,128)(2,1)S(1)}, bf16[192,576]{1,0:T(8,128)(2,1)S(1)}, u32[]{:S(2)}, u32[]{:S(2)}) collective-permute-start(bf16[192,576]{1,0:T(8,128)(2,1)S(1)} %copy-done.16), channel_id=1, source_target_pairs={{0,32},{16,48},{32,0},{48,16},{64,96},{80,112},{96,64},{112,80},{1... | collective-permute-start | bytes 663560 | tf_op jit(solution)/shard_map/ppermute | solution.py:333
  154.3 5.2 %collective-permute-start.15 = (bf16[192,576]{1,0:T(8,128)(2,1)S(1)}, bf16[192,576]{1,0:T(8,128)(2,1)S(1)}, u32[]{:S(2)}, u32[]{:S(2)}) collective-permute-start(bf16[192,576]{1,0:T(8,128)(2,1)S(1)} %copy-done.15), channel_id=1, source_target_pairs={{0,48},{16,0},{32,16},{48,32},{64,112},{80,64},{96,80},{112,96},{1... | collective-permute-start | bytes 663560 | tf_op jit(solution)/shard_map/ppermute | solution.py:333
  160.3 5.8 %all-to-all-start.4 = ((bf16[8,48,128]{2,1,0:T(8,128)(2,1)}), bf16[8,48,128]{2,1,0:T(8,128)(2,1)S(1)}, u32[]{:S(2)}, u32[]{:S(2)}) async-start(bf16[8,48,128]{2,1,0:T(8,128)(2,1)} %bitcast.13), calls=%async_computation.4 | async-start | bytes 196608 | tf_op jit(solution)/shard_map/all_to_all | solution.py:324
  166.0 3.3 %shard_map.113 = bf16[1,192,1536]{2,1,0:T(8,128)(2,1)} custom-call(bf16[768,1536]{1,0:T(8,128)(2,1)} %get-tuple-element.82.weight, bf16[768,192]{1,0:T(8,128)(2,1)} %bitcast.23), custom_call_target="tpu_custom_call" | custom-call | flops 452984832 | bytes 3244032 | tf_op jit(solution)/shard_map/pallas_call | solution.py:41
  169.3 5.1 %collective-permute-done.14.refs_2_ = bf16[192,576]{1,0:T(8,128)(2,1)S(1)} collective-permute-done((bf16[192,576]{1,0:T(8,128)(2,1)S(1)}, bf16[192,576]{1,0:T(8,128)(2,1)S(1)}, u32[]{:S(2)}, u32[]{:S(2)}) %collective-permute-start.14) | collective-permute-done | bytes 221216 | tf_op jit(solution)/shard_map/ppermute | solution.py:333
  174.4 3.8 %collective-permute-done.15.refs_3_ = bf16[192,576]{1,0:T(8,128)(2,1)S(1)} collective-permute-done((bf16[192,576]{1,0:T(8,128)(2,1)S(1)}, bf16[192,576]{1,0:T(8,128)(2,1)S(1)}, u32[]{:S(2)}, u32[]{:S(2)}) %collective-permute-start.15) | collective-permute-done | bytes 221216 | tf_op jit(solution)/shard_map/ppermute | solution.py:333
  (68 shorter events, 24.7 us)
Async XLA Ops:
  0.6 6.8 %collective-permute-start = (bf16[48,1536]{1,0:T(8,128)(2,1)}, bf16[48,1536]{1,0:T(8,128)(2,1)S(1)}, u32[]{:S(2)}, u32[]{:S(2)}) collective-permute-start(bf16[48,1536]{1,0:T(8,128)(2,1)} %refs_0_.1), channel_id=1, source_target_pairs={{0,2},{1,3},{2,0},{3,1},{4,6},{5,7},{6,4},{7,5},{8,10},{9,11},{10,... | collective-permute-start | bytes 442376 | tf_op jit(solution)/shard_map/ppermute | solution.py:339
  7.0 8.1 %copy-start.2 = (bf16[48,1536]{1,0:T(8,128)(2,1)S(1)}, bf16[48,1536]{1,0:T(8,128)(2,1)}, u32[]{:S(2)}) copy-start(bf16[48,1536]{1,0:T(8,128)(2,1)} %refs_0_.1) | copy-start | bytes 442372
  7.4 32.1 %all-to-all-start = ((bf16[4,192,576]{2,1,0:T(8,128)(2,1)}), bf16[4,192,576]{2,1,0:T(8,128)(2,1)S(1)}, u32[]{:S(2)}, u32[]{:S(2)}) async-start(bf16[4,192,576]{2,1,0:T(8,128)(2,1)} %bitcast.21), calls=%async_computation | async-start | bytes 1966080 | tf_op jit(solution)/shard_map/all_to_all | solution.py:324
  15.1 9.6 %collective-permute-start.3 = (bf16[96,1536]{1,0:T(8,128)(2,1)S(1)}, bf16[96,1536]{1,0:T(8,128)(2,1)S(1)}, u32[]{:S(2)}, u32[]{:S(2)}) collective-permute-start(bf16[96,1536]{1,0:T(8,128)(2,1)S(1)} %shard_map.102.refs_0_), channel_id=1, source_target_pairs={{0,12},{1,13},{2,14},{3,15},{4,0},{5,1},{6,2},{7,3},{8,4},{9,5},{1... | collective-permute-start | bytes 884744 | tf_op jit(solution)/shard_map/ppermute | solution.py:336
  19.5 9.8 %collective-permute-start.2 = (bf16[96,1536]{1,0:T(8,128)(2,1)S(1)}, bf16[96,1536]{1,0:T(8,128)(2,1)S(1)}, u32[]{:S(2)}, u32[]{:S(2)}) collective-permute-start(bf16[96,1536]{1,0:T(8,128)(2,1)S(1)} %shard_map.102.refs_0_), channel_id=1, source_target_pairs={{0,8},{1,9},{2,10},{3,11},{4,12},{5,13},{6,14},{7,15},{8,0},{9,1},... | collective-permute-start | bytes 884744 | tf_op jit(solution)/shard_map/ppermute | solution.py:336
  22.0 15.6 %collective-permute-start.1 = (bf16[96,1536]{1,0:T(8,128)(2,1)S(1)}, bf16[96,1536]{1,0:T(8,128)(2,1)S(1)}, u32[]{:S(2)}, u32[]{:S(2)}) collective-permute-start(bf16[96,1536]{1,0:T(8,128)(2,1)S(1)} %shard_map.102.refs_0_), channel_id=1, source_target_pairs={{0,4},{1,5},{2,6},{3,7},{4,8},{5,9},{6,10},{7,11},{8,12},{9,13},{1... | collective-permute-start | bytes 884744 | tf_op jit(solution)/shard_map/ppermute | solution.py:336
  39.6 10.0 %collective-permute-start.4 = (bf16[384,384]{1,0:T(8,128)(2,1)S(1)}, bf16[384,384]{1,0:T(8,128)(2,1)S(1)}, u32[]{:S(2)}, u32[]{:S(2)}) collective-permute-start(bf16[384,384]{1,0:T(8,128)(2,1)S(1)} %get-tuple-element.75), channel_id=1, source_target_pairs={{0,64},{16,80},{32,96},{48,112},{64,128},{80,144},{96,160},{112,17... | collective-permute-start | bytes 884744 | tf_op jit(solution)/shard_map/ppermute | solution.py:329
  43.8 10.5 %collective-permute-start.5 = (bf16[384,384]{1,0:T(8,128)(2,1)S(1)}, bf16[384,384]{1,0:T(8,128)(2,1)S(1)}, u32[]{:S(2)}, u32[]{:S(2)}) collective-permute-start(bf16[384,384]{1,0:T(8,128)(2,1)S(1)} %get-tuple-element.76), channel_id=1, source_target_pairs={{64,0},{80,16},{96,32},{112,48},{128,64},{144,80},{160,96},{176,11... | collective-permute-start | bytes 884744 | tf_op jit(solution)/shard_map/ppermute | solution.py:329
  45.2 20.0 %copy-start = (bf16[384,1536]{1,0:T(8,128)(2,1)}, bf16[384,1536]{1,0:T(8,128)(2,1)S(1)}, u32[]{:S(2)}) copy-start(bf16[384,1536]{1,0:T(8,128)(2,1)S(1)} %shard_map.103.mine) | copy-start | bytes 3538948
  54.3 15.1 %collective-permute-start.6 = (bf16[384,1536]{1,0:T(8,128)(2,1)S(1)}, bf16[384,1536]{1,0:T(8,128)(2,1)S(1)}, u32[]{:S(2)}, u32[]{:S(2)}) collective-permute-start(bf16[384,1536]{1,0:T(8,128)(2,1)S(1)} %shard_map.103.mine), channel_id=1, source_target_pairs={{0,1},{1,0},{2,3},{3,2},{4,5},{5,4},{6,7},{7,6},{8,9},{9,8},{10,11... | collective-permute-start | bytes 3538952 | tf_op jit(solution)/shard_map/ppermute | solution.py:342
  65.2 23.5 %all-to-all-start.1 = ((bf16[4,192,192]{2,1,0:T(8,128)(2,1)}), bf16[4,192,192]{2,1,0:T(8,128)(2,1)S(1)}, u32[]{:S(2)}, u32[]{:S(2)}) async-start(bf16[4,192,192]{2,1,0:T(8,128)(2,1)} %bitcast.24), calls=%async_computation.1 | async-start | bytes 786432 | tf_op jit(solution)/shard_map/all_to_all | solution.py:324
  74.0 14.7 %collective-permute-start.7 = (bf16[192,192]{1,0:T(8,128)(2,1)}, bf16[192,192]{1,0:T(8,128)(2,1)S(1)}, u32[]{:S(2)}, u32[]{:S(2)}) collective-permute-start(bf16[192,192]{1,0:T(8,128)(2,1)} %get-tuple-element.84), channel_id=1, source_target_pairs={{0,16},{16,32},{32,48},{48,0},{64,80},{80,96},{96,112},{112,64},{1... | collective-permute-start | bytes 221192 | tf_op jit(solution)/shard_map/ppermute | solution.py:333
  78.2 10.5 %collective-permute-start.8 = (bf16[192,192]{1,0:T(8,128)(2,1)}, bf16[192,192]{1,0:T(8,128)(2,1)S(1)}, u32[]{:S(2)}, u32[]{:S(2)}) collective-permute-start(bf16[192,192]{1,0:T(8,128)(2,1)} %get-tuple-element.85), channel_id=1, source_target_pairs={{0,32},{16,48},{32,0},{48,16},{64,96},{80,112},{96,64},{112,80},{1... | collective-permute-start | bytes 221192 | tf_op jit(solution)/shard_map/ppermute | solution.py:333
  83.5 9.7 %collective-permute-start.9 = (bf16[192,192]{1,0:T(8,128)(2,1)}, bf16[192,192]{1,0:T(8,128)(2,1)S(1)}, u32[]{:S(2)}, u32[]{:S(2)}) collective-permute-start(bf16[192,192]{1,0:T(8,128)(2,1)} %get-tuple-element.86), channel_id=1, source_target_pairs={{0,48},{16,0},{32,16},{48,32},{64,112},{80,64},{96,80},{112,96},{1... | collective-permute-start | bytes 221192 | tf_op jit(solution)/shard_map/ppermute | solution.py:333
  88.7 11.5 %copy-start.18 = (bf16[192,192]{1,0:T(8,128)(2,1)}, bf16[192,192]{1,0:T(8,128)(2,1)S(1)}, u32[]{:S(2)}) copy-start(bf16[192,192]{1,0:T(8,128)(2,1)S(1)} %collective-permute-done.7.refs_8_) | copy-start | bytes 221188
  88.7 11.5 %copy-start.19 = (bf16[192,192]{1,0:T(8,128)(2,1)}, bf16[192,192]{1,0:T(8,128)(2,1)S(1)}, u32[]{:S(2)}) copy-start(bf16[192,192]{1,0:T(8,128)(2,1)S(1)} %collective-permute-done.8.refs_9_) | copy-start | bytes 221188
  93.1 7.1 %copy-start.20 = (bf16[192,192]{1,0:T(8,128)(2,1)}, bf16[192,192]{1,0:T(8,128)(2,1)S(1)}, u32[]{:S(2)}) copy-start(bf16[192,192]{1,0:T(8,128)(2,1)S(1)} %collective-permute-done.9.refs_10_) | copy-start | bytes 221188
  97.4 12.6 %collective-permute-start.10 = (bf16[384,1536]{1,0:T(8,128)(2,1)}, bf16[384,1536]{1,0:T(8,128)(2,1)S(1)}, u32[]{:S(2)}, u32[]{:S(2)}) collective-permute-start(bf16[384,1536]{1,0:T(8,128)(2,1)} %get-tuple-element.94), channel_id=1, source_target_pairs={{0,1},{1,0},{2,3},{3,2},{4,5},{5,4},{6,7},{7,6},{8,9},{9,8},{10,11... | collective-permute-start | bytes 3538952 | tf_op jit(solution)/shard_map/ppermute | solution.py:342
  113.9 7.7 %copy-start.13 = (bf16[384,384]{1,0:T(8,128)(2,1)S(1)}, bf16[384,384]{1,0:T(8,128)(2,1)}, u32[]{:S(2)}) copy-start(bf16[384,384]{1,0:T(8,128)(2,1)} %get-tuple-element.110) | copy-start | bytes 884740
  113.9 23.3 %all-to-all-start.2 = ((bf16[4,96,1536]{2,1,0:T(8,128)(2,1)}), bf16[4,96,1536]{2,1,0:T(8,128)(2,1)S(1)}, u32[]{:S(2)}, u32[]{:S(2)}) async-start(bf16[4,96,1536]{2,1,0:T(8,128)(2,1)} %bitcast.20), calls=%async_computation.2 | async-start | bytes 2359296 | tf_op jit(solution)/shard_map/all_to_all | solution.py:324
  117.5 10.2 %collective-permute-start.11 = (bf16[384,384]{1,0:T(8,128)(2,1)S(1)}, bf16[384,384]{1,0:T(8,128)(2,1)S(1)}, u32[]{:S(2)}, u32[]{:S(2)}) collective-permute-start(bf16[384,384]{1,0:T(8,128)(2,1)S(1)} %copy-done.14), channel_id=1, source_target_pairs={{0,64},{16,80},{32,96},{48,112},{64,128},{80,144},{96,160},{112,17... | collective-permute-start | bytes 884744 | tf_op jit(solution)/shard_map/ppermute | solution.py:329
  121.6 12.2 %collective-permute-start.12 = (bf16[384,384]{1,0:T(8,128)(2,1)S(1)}, bf16[384,384]{1,0:T(8,128)(2,1)S(1)}, u32[]{:S(2)}, u32[]{:S(2)}) collective-permute-start(bf16[384,384]{1,0:T(8,128)(2,1)S(1)} %copy-done.13), channel_id=1, source_target_pairs={{64,0},{80,16},{96,32},{112,48},{128,64},{144,80},{160,96},{176,11... | collective-permute-start | bytes 884744 | tf_op jit(solution)/shard_map/ppermute | solution.py:329
  127.8 6.0 %copy-start.6 = (bf16[384,384]{1,0:T(8,128)(2,1)}, bf16[384,384]{1,0:T(8,128)(2,1)S(1)}, u32[]{:S(2)}) copy-start(bf16[384,384]{1,0:T(8,128)(2,1)S(1)} %collective-permute-done.11.from_before) | copy-start | bytes 884740
  137.1 7.7 %copy-start.17 = (bf16[192,576]{1,0:T(8,128)(2,1)S(1)}, bf16[192,576]{1,0:T(8,128)(2,1)}, u32[]{:S(2)}) copy-start(bf16[192,576]{1,0:T(8,128)(2,1)} %get-tuple-element.119) | copy-start | bytes 663556
  137.1 11.9 %copy-start.16 = (bf16[192,576]{1,0:T(8,128)(2,1)S(1)}, bf16[192,576]{1,0:T(8,128)(2,1)}, u32[]{:S(2)}) copy-start(bf16[192,576]{1,0:T(8,128)(2,1)} %get-tuple-element.120) | copy-start | bytes 663556
  137.1 17.1 %copy-start.15 = (bf16[192,576]{1,0:T(8,128)(2,1)S(1)}, bf16[192,576]{1,0:T(8,128)(2,1)}, u32[]{:S(2)}) copy-start(bf16[192,576]{1,0:T(8,128)(2,1)} %get-tuple-element.121) | copy-start | bytes 663556
  138.3 21.2 %all-to-all-start.3 = ((bf16[8,48,384]{2,1,0:T(8,128)(2,1)}), bf16[8,48,384]{2,1,0:T(8,128)(2,1)S(1)}, u32[]{:S(2)}, u32[]{:S(2)}) async-start(bf16[8,48,384]{2,1,0:T(8,128)(2,1)} %bitcast.11), calls=%async_computation.3 | async-start | bytes 589824 | tf_op jit(solution)/shard_map/all_to_all | solution.py:324
  144.8 24.5 %collective-permute-start.13 = (bf16[192,576]{1,0:T(8,128)(2,1)S(1)}, bf16[192,576]{1,0:T(8,128)(2,1)S(1)}, u32[]{:S(2)}, u32[]{:S(2)}) collective-permute-start(bf16[192,576]{1,0:T(8,128)(2,1)S(1)} %copy-done.17), channel_id=1, source_target_pairs={{0,16},{16,32},{32,48},{48,0},{64,80},{80,96},{96,112},{112,64},{1... | collective-permute-start | bytes 663560 | tf_op jit(solution)/shard_map/ppermute | solution.py:333
  149.1 25.3 %collective-permute-start.14 = (bf16[192,576]{1,0:T(8,128)(2,1)S(1)}, bf16[192,576]{1,0:T(8,128)(2,1)S(1)}, u32[]{:S(2)}, u32[]{:S(2)}) collective-permute-start(bf16[192,576]{1,0:T(8,128)(2,1)S(1)} %copy-done.16), channel_id=1, source_target_pairs={{0,32},{16,48},{32,0},{48,16},{64,96},{80,112},{96,64},{112,80},{1... | collective-permute-start | bytes 663560 | tf_op jit(solution)/shard_map/ppermute | solution.py:333
  154.3 23.9 %collective-permute-start.15 = (bf16[192,576]{1,0:T(8,128)(2,1)S(1)}, bf16[192,576]{1,0:T(8,128)(2,1)S(1)}, u32[]{:S(2)}, u32[]{:S(2)}) collective-permute-start(bf16[192,576]{1,0:T(8,128)(2,1)S(1)} %copy-done.15), channel_id=1, source_target_pairs={{0,48},{16,0},{32,16},{48,32},{64,112},{80,64},{96,80},{112,96},{1... | collective-permute-start | bytes 663560 | tf_op jit(solution)/shard_map/ppermute | solution.py:333
  160.3 21.4 %all-to-all-start.4 = ((bf16[8,48,128]{2,1,0:T(8,128)(2,1)}), bf16[8,48,128]{2,1,0:T(8,128)(2,1)S(1)}, u32[]{:S(2)}, u32[]{:S(2)}) async-start(bf16[8,48,128]{2,1,0:T(8,128)(2,1)} %bitcast.13), calls=%async_computation.4 | async-start | bytes 196608 | tf_op jit(solution)/shard_map/all_to_all | solution.py:324
  169.3 8.9 %copy-start.8 = (bf16[192,576]{1,0:T(8,128)(2,1)}, bf16[192,576]{1,0:T(8,128)(2,1)S(1)}, u32[]{:S(2)}) copy-start(bf16[192,576]{1,0:T(8,128)(2,1)S(1)} %collective-permute-done.13.refs_1_) | copy-start | bytes 663556
  (10 other events, 29.2 us)

commit v3 on v2

--- a/solution.py
+++ b/solution.py
@@ -407,7 +407,12 @@
     received, low, high = together((received, low, high))
     from_after, from_before = along_z(low, -1), along_z(high, 1)
     sums = call(add_cores, half, (keep, received), smem=0)
+    sums, context_rows = together((sums, context_rows))
     sums = exchange(sums, "fsdp", x_groups)
+    attended = call(
+        project, struct((1, ROWS, WIDTH)), (weight, context_rows), flops=project_flops, smem=0
+    )
+    attended, from_after = together((attended, from_after))
     chunks = call(
         pack_grads,
         (chunk,) * GROUP,
@@ -419,12 +424,7 @@
     grads = spread(chunks)
     sums = exchange(sums, ("seq", "fsdp"), whole_y_groups)
     sums = call(add_y, struct((n_z * STRIP, 128)), (sums,), smem=0, near=True)
-    sums, context_rows = together((sums, context_rows))
     sums = exchange(sums, "seq", z_groups)
-    attended = call(
-        project, struct((1, ROWS, WIDTH)), (weight, context_rows), flops=project_flops, smem=0
-    )
-    attended, grads = together((attended, grads))
     grad_queries, grad_keys, grad_values = call(unpack_grads, (full, full, full), (pos, *grads))
     sums, grad_queries = together((sums, grad_queries))
     grad_weight = call(add_z, struct((STRIP, STRIP), F32), (sums,), smem=0, near=True)

time: 183 us -> 181 us (0.989)
  waiting for transfers between devices: 48.7 us -> 39.2 us
  starting transfers between devices: 87.6 us -> 93.8 us
    ppermute x4, waiting for transfers between devices: 19.9 us -> 12 us  [along_z(): return lax.ppermute(block, 'seq', route)]
    all_to_all x5, starting transfers between devices: 27.9 us -> 33.5 us  [exchange(): lax.all_to_all(block, axis, 0, 0, axis_index_groups=groups, tiled=True)]
    ppermute x6, waiting for transfers between devices: 13.3 us -> 11 us  [along_y(): return lax.ppermute(block, 'seq', route)]
  transfers between devices with their start and end apart: 21 -> 21, of which waited for: 12 -> 13; matrix products, arithmetic and copies ran while one was open for 0% -> 0% of each run, Pallas kernels for 17% -> 18%
where the time goes in v3:
time: 181 us; the launch traced here: 179 us
  starting transfers between devices  93.8 us (52%)
  Pallas kernels  40.8 us (23%)
  waiting for transfers between devices  39.2 us (22%)
  local copies, waits for them, and re-layouts  4.15 us (2%)
    pallas_call x15, Pallas kernels, call(): pl.pallas_call(body, out_shape=out_shape, grid=() if near else (1,), in_s...  40.8 us
    all_to_all x5, starting transfers between devices, exchange(): lax.all_to_all(block, axis, 0, 0, axis_index_groups=groups, tiled=True)  33.5 us
    ppermute x6, starting transfers between devices, along_y(): return lax.ppermute(block, 'seq', route)  29.3 us
    ppermute x3, waiting for transfers between devices, along_x(): lax.ppermute(block, 'fsdp', [(i, (i + 4 * hop) % 16) for i in range(16)])  13.1 us
    ppermute x4, waiting for transfers between devices, along_z(): return lax.ppermute(block, 'seq', route)  12 us
    ppermute x4, starting transfers between devices, along_z(): return lax.ppermute(block, 'seq', route)  11.5 us
    ppermute x6, waiting for transfers between devices, along_y(): return lax.ppermute(block, 'seq', route)  11 us
    ppermute x3, starting transfers between devices, along_x(): lax.ppermute(block, 'fsdp', [(i, (i + 4 * hop) % 16) for i in range(16)])  9.33 us
  transfers between devices with their start and end apart: 21, of which 13 were waited for; matrix products, arithmetic and copies ran while one was open for 0% of the time, Pallas kernels for 18%

profile of v3, /device:TPU:1, one launch (start us, length us, event | category | flops | bytes accessed | tf_op | source)
XLA Modules:
  0.0 179.1 jit_solution(2927521478295905307)
XLA Ops:
  0.6 4.0 %collective-permute-start = (bf16[48,1536]{1,0:T(8,128)(2,1)}, bf16[48,1536]{1,0:T(8,128)(2,1)S(1)}, u32[]{:S(2)}, u32[]{:S(2)}) collective-permute-start(bf16[48,1536]{1,0:T(8,128)(2,1)} %refs_0_.1), channel_id=1, source_target_pairs={{0,2},{1,3},{2,0},{3,1},{4,6},{5,7},{6,4},{7,5},{8,10},{9,11},{10,... | collective-permute-start | bytes 442376 | tf_op jit(solution)/shard_map/ppermute | solution.py:339
  7.4 7.7 %all-to-all-start = ((bf16[4,192,576]{2,1,0:T(8,128)(2,1)}), bf16[4,192,576]{2,1,0:T(8,128)(2,1)S(1)}, u32[]{:S(2)}, u32[]{:S(2)}) async-start(bf16[4,192,576]{2,1,0:T(8,128)(2,1)} %bitcast.21), calls=%async_computation | async-start | bytes 1966080 | tf_op jit(solution)/shard_map/all_to_all | solution.py:324
  15.1 4.4 %collective-permute-start.3 = (bf16[96,1536]{1,0:T(8,128)(2,1)S(1)}, bf16[96,1536]{1,0:T(8,128)(2,1)S(1)}, u32[]{:S(2)}, u32[]{:S(2)}) collective-permute-start(bf16[96,1536]{1,0:T(8,128)(2,1)S(1)} %shard_map.102.refs_0_), channel_id=1, source_target_pairs={{0,12},{1,13},{2,14},{3,15},{4,0},{5,1},{6,2},{7,3},{8,4},{9,5},{1... | collective-permute-start | bytes 884744 | tf_op jit(solution)/shard_map/ppermute | solution.py:336
  24.8 4.5 %collective-permute-done.2.refs_2_ = bf16[96,1536]{1,0:T(8,128)(2,1)S(1)} collective-permute-done((bf16[96,1536]{1,0:T(8,128)(2,1)S(1)}, bf16[96,1536]{1,0:T(8,128)(2,1)S(1)}, u32[]{:S(2)}, u32[]{:S(2)}) %collective-permute-start.2) | collective-permute-done | bytes 294944 | tf_op jit(solution)/shard_map/ppermute | solution.py:336
  29.3 8.2 %collective-permute-done.1.refs_1_ = bf16[96,1536]{1,0:T(8,128)(2,1)S(1)} collective-permute-done((bf16[96,1536]{1,0:T(8,128)(2,1)S(1)}, bf16[96,1536]{1,0:T(8,128)(2,1)S(1)}, u32[]{:S(2)}, u32[]{:S(2)}) %collective-permute-start.1) | collective-permute-done | bytes 294944 | tf_op jit(solution)/shard_map/ppermute | solution.py:336
  39.6 4.2 %collective-permute-start.4 = (bf16[384,384]{1,0:T(8,128)(2,1)S(1)}, bf16[384,384]{1,0:T(8,128)(2,1)S(1)}, u32[]{:S(2)}, u32[]{:S(2)}) collective-permute-start(bf16[384,384]{1,0:T(8,128)(2,1)S(1)} %get-tuple-element.72), channel_id=1, source_target_pairs={{0,64},{16,80},{32,96},{48,112},{64,128},{80,144},{96,160},{112,17... | collective-permute-start | bytes 884744 | tf_op jit(solution)/shard_map/ppermute | solution.py:329
  45.3 4.3 %collective-permute-done.4.refs_3_ = bf16[384,384]{1,0:T(8,128)(2,1)S(1)} collective-permute-done((bf16[384,384]{1,0:T(8,128)(2,1)S(1)}, bf16[384,384]{1,0:T(8,128)(2,1)S(1)}, u32[]{:S(2)}, u32[]{:S(2)}) %collective-permute-start.4) | collective-permute-done | bytes 294944 | tf_op jit(solution)/shard_map/ppermute | solution.py:329
  49.6 4.8 %collective-permute-done.5.refs_4_ = bf16[384,384]{1,0:T(8,128)(2,1)S(1)} collective-permute-done((bf16[384,384]{1,0:T(8,128)(2,1)S(1)}, bf16[384,384]{1,0:T(8,128)(2,1)S(1)}, u32[]{:S(2)}, u32[]{:S(2)}) %collective-permute-start.5) | collective-permute-done | bytes 294944 | tf_op jit(solution)/shard_map/ppermute | solution.py:329
  54.3 3.4 %collective-permute-start.6 = (bf16[384,1536]{1,0:T(8,128)(2,1)S(1)}, bf16[384,1536]{1,0:T(8,128)(2,1)S(1)}, u32[]{:S(2)}, u32[]{:S(2)}) collective-permute-start(bf16[384,1536]{1,0:T(8,128)(2,1)S(1)} %shard_map.103.mine), channel_id=1, source_target_pairs={{0,1},{1,0},{2,3},{3,2},{4,5},{5,4},{6,7},{7,6},{8,9},{9,8},{10,11... | collective-permute-start | bytes 3538952 | tf_op jit(solution)/shard_map/ppermute | solution.py:342
  58.4 6.8 %shard_map.105 = (bf16[768,192]{1,0:T(8,128)(2,1)}, bf16[1536,192]{1,0:T(8,128)(2,1)}, bf16[1536,192]{1,0:T(8,128)(2,1)}, bf16[768,192]{1,0:T(8,128)(2,1)}, f32[768,128]{1,0:T(8,128)}) custom-call(s32[5]{0:T(128)} %stack.23.refs_0_.pos, s32[1,4]{1,0:T(1,128)} %refs_1_.3, bf16[768,576]{1,0:T(8,128)(2,1)} %bitcast.17, bf16[384,384]{1,0:T(8,128)(2,1)} %copy-done.11, ...), custom_call_target="tpu_custom_call" | custom-call | flops 1207959552 | bytes 3637284 | tf_op jit(solution)/shard_map/pallas_call | solution.py:41
  65.2 4.3 %all-to-all-start.1 = ((bf16[4,192,192]{2,1,0:T(8,128)(2,1)}), bf16[4,192,192]{2,1,0:T(8,128)(2,1)S(1)}, u32[]{:S(2)}, u32[]{:S(2)}) async-start(bf16[4,192,192]{2,1,0:T(8,128)(2,1)} %bitcast.24), calls=%async_computation.1 | async-start | bytes 786432 | tf_op jit(solution)/shard_map/all_to_all | solution.py:324
  70.5 3.5 %shard_map.106 = (bf16[768,1536]{1,0:T(8,128)(2,1)}, bf16[192,192]{1,0:T(8,128)(2,1)}, bf16[192,192]{1,0:T(8,128)(2,1)}, bf16[192,192]{1,0:T(8,128)(2,1)}, bf16[192,192]{1,0:T(8,128)(2,1)}) custom-call(s32[5]{0:T(128)} %stack.23.refs_0_.pos, bf16[1,192,1536]{2,1,0:T(8,128)(2,1)} %cot.3, bf16[384,1536]{1,0:T(8,128)(2,1)} %copy-done, bf16[384,1536]{1,0:T(8,128)(2,1)} %copy-done.4), custom_call_target="tpu_custom_call" | custom-call | flops 452984832 | bytes 5603348 | tf_op jit(solution)/shard_map/pallas_call | solution.py:41
  74.0 4.3 %collective-permute-start.7 = (bf16[192,192]{1,0:T(8,128)(2,1)}, bf16[192,192]{1,0:T(8,128)(2,1)S(1)}, u32[]{:S(2)}, u32[]{:S(2)}) collective-permute-start(bf16[192,192]{1,0:T(8,128)(2,1)} %get-tuple-element.81), channel_id=1, source_target_pairs={{0,16},{16,32},{32,48},{48,0},{64,80},{80,96},{96,112},{112,64},{1... | collective-permute-start | bytes 221192 | tf_op jit(solution)/shard_map/ppermute | solution.py:333
  78.2 5.2 %collective-permute-start.8 = (bf16[192,192]{1,0:T(8,128)(2,1)}, bf16[192,192]{1,0:T(8,128)(2,1)S(1)}, u32[]{:S(2)}, u32[]{:S(2)}) collective-permute-start(bf16[192,192]{1,0:T(8,128)(2,1)} %get-tuple-element.82), channel_id=1, source_target_pairs={{0,32},{16,48},{32,0},{48,16},{64,96},{80,112},{96,64},{112,80},{1... | collective-permute-start | bytes 221192 | tf_op jit(solution)/shard_map/ppermute | solution.py:333
  83.5 5.2 %collective-permute-start.9 = (bf16[192,192]{1,0:T(8,128)(2,1)}, bf16[192,192]{1,0:T(8,128)(2,1)S(1)}, u32[]{:S(2)}, u32[]{:S(2)}) collective-permute-start(bf16[192,192]{1,0:T(8,128)(2,1)} %get-tuple-element.83), channel_id=1, source_target_pairs={{0,48},{16,0},{32,16},{48,32},{64,112},{80,64},{96,80},{112,96},{1... | collective-permute-start | bytes 221192 | tf_op jit(solution)/shard_map/ppermute | solution.py:333
  88.7 4.4 %collective-permute-done.9.refs_10_ = bf16[192,192]{1,0:T(8,128)(2,1)S(1)} collective-permute-done((bf16[192,192]{1,0:T(8,128)(2,1)}, bf16[192,192]{1,0:T(8,128)(2,1)S(1)}, u32[]{:S(2)}, u32[]{:S(2)}) %collective-permute-start.9) | collective-permute-done | bytes 73760 | tf_op jit(solution)/shard_map/ppermute | solution.py:333
  93.1 4.3 %shard_map.107 = (bf16[384,1536]{1,0:T(8,128)(2,1)}, bf16[384,1536]{1,0:T(8,128)(2,1)}) custom-call(s32[5]{0:T(128)} %stack.23.refs_0_.pos, bf16[1,192,1536]{2,1,0:T(8,128)(2,1)} %cot.3, bf16[768,192]{1,0:T(8,128)(2,1)} %bitcast.22), custom_call_target="tpu_custom_call" | custom-call | flops 452984832 | bytes 3244052 | tf_op jit(solution)/shard_map/pallas_call | solution.py:41
  97.4 2.8 %collective-permute-start.10 = (bf16[384,1536]{1,0:T(8,128)(2,1)}, bf16[384,1536]{1,0:T(8,128)(2,1)S(1)}, u32[]{:S(2)}, u32[]{:S(2)}) collective-permute-start(bf16[384,1536]{1,0:T(8,128)(2,1)} %get-tuple-element.91), channel_id=1, source_target_pairs={{0,1},{1,0},{2,3},{3,2},{4,5},{5,4},{6,7},{7,6},{8,9},{9,8},{10,11... | collective-permute-start | bytes 3538952 | tf_op jit(solution)/shard_map/ppermute | solution.py:342
  100.3 9.7 %shard_map.108 = (bf16[768,192]{1,0:T(8,128)(2,1)}, f32[768,384]{1,0:T(8,128)}, bf16[384,384]{1,0:T(8,128)(2,1)}, bf16[384,384]{1,0:T(8,128)(2,1)}) custom-call(s32[5]{0:T(128)} %stack.23.refs_0_.pos, s32[1,4]{1,0:T(1,128)} %refs_1_.3, bf16[768,192]{1,0:T(8,128)(2,1)} %get-tuple-element.92.refs_2_, bf16[1536,192]{1,0:T(8,128)(2,1)} %get-tuple-element.93.refs_3_, ...), custom_call_target="tpu_custom_call" | custom-call | flops 3019898880 | bytes 4522020 | tf_op jit(solution)/shard_map/pallas_call | solution.py:41
  110.9 2.9 %shard_map.109 = bf16[384,1536]{1,0:T(8,128)(2,1)} custom-call(bf16[384,1536]{1,0:T(8,128)(2,1)} %get-tuple-element.90.keep, bf16[384,1536]{1,0:T(8,128)(2,1)} %copy-done.5), custom_call_target="tpu_custom_call" | custom-call | bytes 3538944 | tf_op jit(solution)/shard_map/pallas_call | solution.py:41
  113.9 3.7 %all-to-all-start.2 = ((bf16[4,96,1536]{2,1,0:T(8,128)(2,1)}), bf16[4,96,1536]{2,1,0:T(8,128)(2,1)S(1)}, u32[]{:S(2)}, u32[]{:S(2)}) async-start(bf16[4,96,1536]{2,1,0:T(8,128)(2,1)} %bitcast.20), calls=%async_computation.2 | async-start | bytes 2359296 | tf_op jit(solution)/shard_map/all_to_all | solution.py:324
  118.9 4.6 %collective-permute-start.12 = (bf16[384,384]{1,0:T(8,128)(2,1)S(1)}, bf16[384,384]{1,0:T(8,128)(2,1)S(1)}, u32[]{:S(2)}, u32[]{:S(2)}) collective-permute-start(bf16[384,384]{1,0:T(8,128)(2,1)S(1)} %copy-done.13), channel_id=1, source_target_pairs={{0,64},{16,80},{32,96},{48,112},{64,128},{80,144},{96,160},{112,17... | collective-permute-start | bytes 884744 | tf_op jit(solution)/shard_map/ppermute | solution.py:329
  123.5 3.3 %shard_map.110 = bf16[1,192,1536]{2,1,0:T(8,128)(2,1)} custom-call(bf16[768,1536]{1,0:T(8,128)(2,1)} %get-tuple-element.79.weight, bf16[768,192]{1,0:T(8,128)(2,1)} %bitcast.23), custom_call_target="tpu_custom_call" | custom-call | flops 452984832 | bytes 3244032 | tf_op jit(solution)/shard_map/pallas_call | solution.py:41
  130.4 2.7 %shard_map.111 = (bf16[192,576]{1,0:T(8,128)(2,1)}, bf16[192,576]{1,0:T(8,128)(2,1)}, bf16[192,576]{1,0:T(8,128)(2,1)}, bf16[192,576]{1,0:T(8,128)(2,1)}) custom-call(s32[5]{0:T(128)} %stack.23.refs_0_.pos, bf16[768,192]{1,0:T(8,128)(2,1)} %get-tuple-element.109.dq, f32[768,384]{1,0:T(8,128)} %get-tuple-element.110.own, bf16[384,384]{1,0:T(8,128)(2,1)} %copy-done.7, ...), custom_call_target="tpu_custom_call" | custom-call | bytes 2949140 | tf_op jit(solution)/shard_map/pallas_call | solution.py:41
  135.0 6.6 %all-to-all-start.3 = ((bf16[8,48,384]{2,1,0:T(8,128)(2,1)}), bf16[8,48,384]{2,1,0:T(8,128)(2,1)S(1)}, u32[]{:S(2)}, u32[]{:S(2)}) async-start(bf16[8,48,384]{2,1,0:T(8,128)(2,1)} %bitcast.11), calls=%async_computation.3 | async-start | bytes 589824 | tf_op jit(solution)/shard_map/all_to_all | solution.py:324
  141.6 4.3 %collective-permute-start.13 = (bf16[192,576]{1,0:T(8,128)(2,1)S(1)}, bf16[192,576]{1,0:T(8,128)(2,1)S(1)}, u32[]{:S(2)}, u32[]{:S(2)}) collective-permute-start(bf16[192,576]{1,0:T(8,128)(2,1)S(1)} %copy-done.17), channel_id=1, source_target_pairs={{0,16},{16,32},{32,48},{48,0},{64,80},{80,96},{96,112},{112,64},{1... | collective-permute-start | bytes 663560 | tf_op jit(solution)/shard_map/ppermute | solution.py:333
  145.9 5.2 %collective-permute-start.14 = (bf16[192,576]{1,0:T(8,128)(2,1)S(1)}, bf16[192,576]{1,0:T(8,128)(2,1)S(1)}, u32[]{:S(2)}, u32[]{:S(2)}) collective-permute-start(bf16[192,576]{1,0:T(8,128)(2,1)S(1)} %copy-done.16), channel_id=1, source_target_pairs={{0,32},{16,48},{32,0},{48,16},{64,96},{80,112},{96,64},{112,80},{1... | collective-permute-start | bytes 663560 | tf_op jit(solution)/shard_map/ppermute | solution.py:333
  151.1 5.2 %collective-permute-start.15 = (bf16[192,576]{1,0:T(8,128)(2,1)S(1)}, bf16[192,576]{1,0:T(8,128)(2,1)S(1)}, u32[]{:S(2)}, u32[]{:S(2)}) collective-permute-start(bf16[192,576]{1,0:T(8,128)(2,1)S(1)} %copy-done.15), channel_id=1, source_target_pairs={{0,48},{16,0},{32,16},{48,32},{64,112},{80,64},{96,80},{112,96},{1... | collective-permute-start | bytes 663560 | tf_op jit(solution)/shard_map/ppermute | solution.py:333
  157.1 11.3 %all-to-all-start.4 = ((bf16[8,48,128]{2,1,0:T(8,128)(2,1)}), bf16[8,48,128]{2,1,0:T(8,128)(2,1)S(1)}, u32[]{:S(2)}, u32[]{:S(2)}) async-start(bf16[8,48,128]{2,1,0:T(8,128)(2,1)} %bitcast.13), calls=%async_computation.4 | async-start | bytes 196608 | tf_op jit(solution)/shard_map/all_to_all | solution.py:324
  168.4 2.8 %collective-permute-done.14.refs_2_ = bf16[192,576]{1,0:T(8,128)(2,1)S(1)} collective-permute-done((bf16[192,576]{1,0:T(8,128)(2,1)S(1)}, bf16[192,576]{1,0:T(8,128)(2,1)S(1)}, u32[]{:S(2)}, u32[]{:S(2)}) %collective-permute-start.14) | collective-permute-done | bytes 221216 | tf_op jit(solution)/shard_map/ppermute | solution.py:333
  171.2 3.9 %collective-permute-done.15.refs_3_ = bf16[192,576]{1,0:T(8,128)(2,1)S(1)} collective-permute-done((bf16[192,576]{1,0:T(8,128)(2,1)S(1)}, bf16[192,576]{1,0:T(8,128)(2,1)S(1)}, u32[]{:S(2)}, u32[]{:S(2)}) %collective-permute-start.15) | collective-permute-done | bytes 221216 | tf_op jit(solution)/shard_map/ppermute | solution.py:333
  175.7 2.7 %shard_map.114 = (bf16[1,192,768]{2,1,0:T(8,128)(2,1)}, bf16[1,192,768]{2,1,0:T(8,128)(2,1)}, bf16[1,192,768]{2,1,0:T(8,128)(2,1)}) custom-call(s32[5]{0:T(128)} %stack.23.refs_0_.pos, bf16[192,576]{1,0:T(8,128)(2,1)} %get-tuple-element.118.refs_0_, bf16[192,576]{1,0:T(8,128)(2,1)} %copy-done.8, bf16[192,576]{1,0:T(8,128)(2,1)} %copy-done.9, ...), custom_call_target="tpu_custom_call" | custom-call | bytes 1769492 | tf_op jit(solution)/shard_map/pallas_call | solution.py:41
  (68 shorter events, 23.1 us)
Async XLA Ops:
  0.6 6.8 %collective-permute-start = (bf16[48,1536]{1,0:T(8,128)(2,1)}, bf16[48,1536]{1,0:T(8,128)(2,1)S(1)}, u32[]{:S(2)}, u32[]{:S(2)}) collective-permute-start(bf16[48,1536]{1,0:T(8,128)(2,1)} %refs_0_.1), channel_id=1, source_target_pairs={{0,2},{1,3},{2,0},{3,1},{4,6},{5,7},{6,4},{7,5},{8,10},{9,11},{10,... | collective-permute-start | bytes 442376 | tf_op jit(solution)/shard_map/ppermute | solution.py:339
  7.0 8.1 %copy-start.2 = (bf16[48,1536]{1,0:T(8,128)(2,1)S(1)}, bf16[48,1536]{1,0:T(8,128)(2,1)}, u32[]{:S(2)}) copy-start(bf16[48,1536]{1,0:T(8,128)(2,1)} %refs_0_.1) | copy-start | bytes 442372
  7.4 32.1 %all-to-all-start = ((bf16[4,192,576]{2,1,0:T(8,128)(2,1)}), bf16[4,192,576]{2,1,0:T(8,128)(2,1)S(1)}, u32[]{:S(2)}, u32[]{:S(2)}) async-start(bf16[4,192,576]{2,1,0:T(8,128)(2,1)} %bitcast.21), calls=%async_computation | async-start | bytes 1966080 | tf_op jit(solution)/shard_map/all_to_all | solution.py:324
  15.1 9.6 %collective-permute-start.3 = (bf16[96,1536]{1,0:T(8,128)(2,1)S(1)}, bf16[96,1536]{1,0:T(8,128)(2,1)S(1)}, u32[]{:S(2)}, u32[]{:S(2)}) collective-permute-start(bf16[96,1536]{1,0:T(8,128)(2,1)S(1)} %shard_map.102.refs_0_), channel_id=1, source_target_pairs={{0,12},{1,13},{2,14},{3,15},{4,0},{5,1},{6,2},{7,3},{8,4},{9,5},{1... | collective-permute-start | bytes 884744 | tf_op jit(solution)/shard_map/ppermute | solution.py:336
  19.5 9.8 %collective-permute-start.2 = (bf16[96,1536]{1,0:T(8,128)(2,1)S(1)}, bf16[96,1536]{1,0:T(8,128)(2,1)S(1)}, u32[]{:S(2)}, u32[]{:S(2)}) collective-permute-start(bf16[96,1536]{1,0:T(8,128)(2,1)S(1)} %shard_map.102.refs_0_), channel_id=1, source_target_pairs={{0,8},{1,9},{2,10},{3,11},{4,12},{5,13},{6,14},{7,15},{8,0},{9,1},... | collective-permute-start | bytes 884744 | tf_op jit(solution)/shard_map/ppermute | solution.py:336
  22.0 15.6 %collective-permute-start.1 = (bf16[96,1536]{1,0:T(8,128)(2,1)S(1)}, bf16[96,1536]{1,0:T(8,128)(2,1)S(1)}, u32[]{:S(2)}, u32[]{:S(2)}) collective-permute-start(bf16[96,1536]{1,0:T(8,128)(2,1)S(1)} %shard_map.102.refs_0_), channel_id=1, source_target_pairs={{0,4},{1,5},{2,6},{3,7},{4,8},{5,9},{6,10},{7,11},{8,12},{9,13},{1... | collective-permute-start | bytes 884744 | tf_op jit(solution)/shard_map/ppermute | solution.py:336
  39.5 5.7 %copy-start.1 = (bf16[4,192,576]{2,1,0:T(8,128)(2,1)}, bf16[4,192,576]{2,1,0:T(8,128)(2,1)S(1)}, u32[]{:S(2)}) copy-start(bf16[4,192,576]{2,1,0:T(8,128)(2,1)S(1)} %all-to-all-done) | copy-start | bytes 2654212
  39.6 10.0 %collective-permute-start.4 = (bf16[384,384]{1,0:T(8,128)(2,1)S(1)}, bf16[384,384]{1,0:T(8,128)(2,1)S(1)}, u32[]{:S(2)}, u32[]{:S(2)}) collective-permute-start(bf16[384,384]{1,0:T(8,128)(2,1)S(1)} %get-tuple-element.72), channel_id=1, source_target_pairs={{0,64},{16,80},{32,96},{48,112},{64,128},{80,144},{96,160},{112,17... | collective-permute-start | bytes 884744 | tf_op jit(solution)/shard_map/ppermute | solution.py:329
  43.8 10.5 %collective-permute-start.5 = (bf16[384,384]{1,0:T(8,128)(2,1)S(1)}, bf16[384,384]{1,0:T(8,128)(2,1)S(1)}, u32[]{:S(2)}, u32[]{:S(2)}) collective-permute-start(bf16[384,384]{1,0:T(8,128)(2,1)S(1)} %get-tuple-element.73), channel_id=1, source_target_pairs={{64,0},{80,16},{96,32},{112,48},{128,64},{144,80},{160,96},{176,11... | collective-permute-start | bytes 884744 | tf_op jit(solution)/shard_map/ppermute | solution.py:329
  45.2 20.0 %copy-start = (bf16[384,1536]{1,0:T(8,128)(2,1)}, bf16[384,1536]{1,0:T(8,128)(2,1)S(1)}, u32[]{:S(2)}) copy-start(bf16[384,1536]{1,0:T(8,128)(2,1)S(1)} %shard_map.103.mine) | copy-start | bytes 3538948
  54.3 15.1 %collective-permute-start.6 = (bf16[384,1536]{1,0:T(8,128)(2,1)S(1)}, bf16[384,1536]{1,0:T(8,128)(2,1)S(1)}, u32[]{:S(2)}, u32[]{:S(2)}) collective-permute-start(bf16[384,1536]{1,0:T(8,128)(2,1)S(1)} %shard_map.103.mine), channel_id=1, source_target_pairs={{0,1},{1,0},{2,3},{3,2},{4,5},{5,4},{6,7},{7,6},{8,9},{9,8},{10,11... | collective-permute-start | bytes 3538952 | tf_op jit(solution)/shard_map/ppermute | solution.py:342
  65.2 23.5 %all-to-all-start.1 = ((bf16[4,192,192]{2,1,0:T(8,128)(2,1)}), bf16[4,192,192]{2,1,0:T(8,128)(2,1)S(1)}, u32[]{:S(2)}, u32[]{:S(2)}) async-start(bf16[4,192,192]{2,1,0:T(8,128)(2,1)} %bitcast.24), calls=%async_computation.1 | async-start | bytes 786432 | tf_op jit(solution)/shard_map/all_to_all | solution.py:324
  74.0 14.7 %collective-permute-start.7 = (bf16[192,192]{1,0:T(8,128)(2,1)}, bf16[192,192]{1,0:T(8,128)(2,1)S(1)}, u32[]{:S(2)}, u32[]{:S(2)}) collective-permute-start(bf16[192,192]{1,0:T(8,128)(2,1)} %get-tuple-element.81), channel_id=1, source_target_pairs={{0,16},{16,32},{32,48},{48,0},{64,80},{80,96},{96,112},{112,64},{1... | collective-permute-start | bytes 221192 | tf_op jit(solution)/shard_map/ppermute | solution.py:333
  78.2 10.5 %collective-permute-start.8 = (bf16[192,192]{1,0:T(8,128)(2,1)}, bf16[192,192]{1,0:T(8,128)(2,1)S(1)}, u32[]{:S(2)}, u32[]{:S(2)}) collective-permute-start(bf16[192,192]{1,0:T(8,128)(2,1)} %get-tuple-element.82), channel_id=1, source_target_pairs={{0,32},{16,48},{32,0},{48,16},{64,96},{80,112},{96,64},{112,80},{1... | collective-permute-start | bytes 221192 | tf_op jit(solution)/shard_map/ppermute | solution.py:333
  83.5 9.7 %collective-permute-start.9 = (bf16[192,192]{1,0:T(8,128)(2,1)}, bf16[192,192]{1,0:T(8,128)(2,1)S(1)}, u32[]{:S(2)}, u32[]{:S(2)}) collective-permute-start(bf16[192,192]{1,0:T(8,128)(2,1)} %get-tuple-element.83), channel_id=1, source_target_pairs={{0,48},{16,0},{32,16},{48,32},{64,112},{80,64},{96,80},{112,96},{1... | collective-permute-start | bytes 221192 | tf_op jit(solution)/shard_map/ppermute | solution.py:333
  88.7 11.5 %copy-start.18 = (bf16[192,192]{1,0:T(8,128)(2,1)}, bf16[192,192]{1,0:T(8,128)(2,1)S(1)}, u32[]{:S(2)}) copy-start(bf16[192,192]{1,0:T(8,128)(2,1)S(1)} %collective-permute-done.7.refs_8_) | copy-start | bytes 221188
  88.7 11.5 %copy-start.19 = (bf16[192,192]{1,0:T(8,128)(2,1)}, bf16[192,192]{1,0:T(8,128)(2,1)S(1)}, u32[]{:S(2)}) copy-start(bf16[192,192]{1,0:T(8,128)(2,1)S(1)} %collective-permute-done.8.refs_9_) | copy-start | bytes 221188
  93.1 7.1 %copy-start.20 = (bf16[192,192]{1,0:T(8,128)(2,1)}, bf16[192,192]{1,0:T(8,128)(2,1)S(1)}, u32[]{:S(2)}) copy-start(bf16[192,192]{1,0:T(8,128)(2,1)S(1)} %collective-permute-done.9.refs_10_) | copy-start | bytes 221188
  97.4 12.6 %collective-permute-start.10 = (bf16[384,1536]{1,0:T(8,128)(2,1)}, bf16[384,1536]{1,0:T(8,128)(2,1)S(1)}, u32[]{:S(2)}, u32[]{:S(2)}) collective-permute-start(bf16[384,1536]{1,0:T(8,128)(2,1)} %get-tuple-element.91), channel_id=1, source_target_pairs={{0,1},{1,0},{2,3},{3,2},{4,5},{5,4},{6,7},{7,6},{8,9},{9,8},{10,11... | collective-permute-start | bytes 3538952 | tf_op jit(solution)/shard_map/ppermute | solution.py:342
  113.9 5.0 %copy-start.13 = (bf16[384,384]{1,0:T(8,128)(2,1)S(1)}, bf16[384,384]{1,0:T(8,128)(2,1)}, u32[]{:S(2)}) copy-start(bf16[384,384]{1,0:T(8,128)(2,1)} %get-tuple-element.111) | copy-start | bytes 884740
  113.9 20.0 %all-to-all-start.2 = ((bf16[4,96,1536]{2,1,0:T(8,128)(2,1)}), bf16[4,96,1536]{2,1,0:T(8,128)(2,1)S(1)}, u32[]{:S(2)}, u32[]{:S(2)}) async-start(bf16[4,96,1536]{2,1,0:T(8,128)(2,1)} %bitcast.20), calls=%async_computation.2 | async-start | bytes 2359296 | tf_op jit(solution)/shard_map/all_to_all | solution.py:324
  117.5 11.3 %collective-permute-start.11 = (bf16[384,384]{1,0:T(8,128)(2,1)S(1)}, bf16[384,384]{1,0:T(8,128)(2,1)S(1)}, u32[]{:S(2)}, u32[]{:S(2)}) collective-permute-start(bf16[384,384]{1,0:T(8,128)(2,1)S(1)} %copy-done.14), channel_id=1, source_target_pairs={{64,0},{80,16},{96,32},{112,48},{128,64},{144,80},{160,96},{176,11... | collective-permute-start | bytes 884744 | tf_op jit(solution)/shard_map/ppermute | solution.py:329
  118.9 10.9 %collective-permute-start.12 = (bf16[384,384]{1,0:T(8,128)(2,1)S(1)}, bf16[384,384]{1,0:T(8,128)(2,1)S(1)}, u32[]{:S(2)}, u32[]{:S(2)}) collective-permute-start(bf16[384,384]{1,0:T(8,128)(2,1)S(1)} %copy-done.13), channel_id=1, source_target_pairs={{0,64},{16,80},{32,96},{48,112},{64,128},{80,144},{96,160},{112,17... | collective-permute-start | bytes 884744 | tf_op jit(solution)/shard_map/ppermute | solution.py:329
  133.1 8.5 %copy-start.17 = (bf16[192,576]{1,0:T(8,128)(2,1)S(1)}, bf16[192,576]{1,0:T(8,128)(2,1)}, u32[]{:S(2)}) copy-start(bf16[192,576]{1,0:T(8,128)(2,1)} %get-tuple-element.119) | copy-start | bytes 663556
  133.1 12.8 %copy-start.16 = (bf16[192,576]{1,0:T(8,128)(2,1)S(1)}, bf16[192,576]{1,0:T(8,128)(2,1)}, u32[]{:S(2)}) copy-start(bf16[192,576]{1,0:T(8,128)(2,1)} %get-tuple-element.120) | copy-start | bytes 663556
  133.1 18.0 %copy-start.15 = (bf16[192,576]{1,0:T(8,128)(2,1)S(1)}, bf16[192,576]{1,0:T(8,128)(2,1)}, u32[]{:S(2)}) copy-start(bf16[192,576]{1,0:T(8,128)(2,1)} %get-tuple-element.121) | copy-start | bytes 663556
  135.0 21.3 %all-to-all-start.3 = ((bf16[8,48,384]{2,1,0:T(8,128)(2,1)}), bf16[8,48,384]{2,1,0:T(8,128)(2,1)S(1)}, u32[]{:S(2)}, u32[]{:S(2)}) async-start(bf16[8,48,384]{2,1,0:T(8,128)(2,1)} %bitcast.11), calls=%async_computation.3 | async-start | bytes 589824 | tf_op jit(solution)/shard_map/all_to_all | solution.py:324
  141.6 26.8 %collective-permute-start.13 = (bf16[192,576]{1,0:T(8,128)(2,1)S(1)}, bf16[192,576]{1,0:T(8,128)(2,1)S(1)}, u32[]{:S(2)}, u32[]{:S(2)}) collective-permute-start(bf16[192,576]{1,0:T(8,128)(2,1)S(1)} %copy-done.17), channel_id=1, source_target_pairs={{0,16},{16,32},{32,48},{48,0},{64,80},{80,96},{96,112},{112,64},{1... | collective-permute-start | bytes 663560 | tf_op jit(solution)/shard_map/ppermute | solution.py:333
  145.9 25.3 %collective-permute-start.14 = (bf16[192,576]{1,0:T(8,128)(2,1)S(1)}, bf16[192,576]{1,0:T(8,128)(2,1)S(1)}, u32[]{:S(2)}, u32[]{:S(2)}) collective-permute-start(bf16[192,576]{1,0:T(8,128)(2,1)S(1)} %copy-done.16), channel_id=1, source_target_pairs={{0,32},{16,48},{32,0},{48,16},{64,96},{80,112},{96,64},{112,80},{1... | collective-permute-start | bytes 663560 | tf_op jit(solution)/shard_map/ppermute | solution.py:333
  151.1 23.9 %collective-permute-start.15 = (bf16[192,576]{1,0:T(8,128)(2,1)S(1)}, bf16[192,576]{1,0:T(8,128)(2,1)S(1)}, u32[]{:S(2)}, u32[]{:S(2)}) collective-permute-start(bf16[192,576]{1,0:T(8,128)(2,1)S(1)} %copy-done.15), channel_id=1, source_target_pairs={{0,48},{16,0},{32,16},{48,32},{64,112},{80,64},{96,80},{112,96},{1... | collective-permute-start | bytes 663560 | tf_op jit(solution)/shard_map/ppermute | solution.py:333
  157.1 21.3 %all-to-all-start.4 = ((bf16[8,48,128]{2,1,0:T(8,128)(2,1)}), bf16[8,48,128]{2,1,0:T(8,128)(2,1)S(1)}, u32[]{:S(2)}, u32[]{:S(2)}) async-start(bf16[8,48,128]{2,1,0:T(8,128)(2,1)} %bitcast.13), calls=%async_computation.4 | async-start | bytes 196608 | tf_op jit(solution)/shard_map/all_to_all | solution.py:324
  168.4 6.6 %copy-start.8 = (bf16[192,576]{1,0:T(8,128)(2,1)}, bf16[192,576]{1,0:T(8,128)(2,1)S(1)}, u32[]{:S(2)}) copy-start(bf16[192,576]{1,0:T(8,128)(2,1)S(1)} %collective-permute-done.13.refs_1_) | copy-start | bytes 663556
  (10 other events, 24.4 us)
